TPU v7x, 256 devices: a whole 4x4x8 slice. The times are simulated.
256 devices in a mesh: frm: 32 (over z_hi, x, core), head: 8 (over z_lo, y).
Axes of the slice: x: 4, y: 4, z: 8 (z_hi: 4, z_lo: 2; z = z_hi * 2 + z_lo), core: 2. Of those that a mesh axis runs over, the one named last changes fastest.
Arguments:
- video_q: bfloat16 [8192, 3072], P('frm', 'head'), may hold values from -8 to 8
- video_k: bfloat16 [8192, 3072], P('frm', 'head'), may hold values from -8 to 8
- video_v: bfloat16 [8192, 3072], P('frm', 'head'), may hold values from -6 to 6
- text_q: bfloat16 [256, 3072], P(None, 'head'), may hold values from -8 to 8
- text_k: bfloat16 [256, 3072], P(None, 'head'), may hold values from -8 to 8
- text_v: bfloat16 [256, 3072], P(None, 'head'), may hold values from -6 to 6
- band_start: int32 [32], P('frm'), may hold values from 0 to 1, as said below
- text_mask: int32 [256], replicated, may hold values 0 or 1
- video_proj: bfloat16 [3072, 3072], P('head'), may hold values from -0.109375 to 0.109375
- text_proj: bfloat16 [3072, 3072], P('head'), may hold values from -0.109375 to 0.109375
Outputs:
- video_out: float32 [8192, 3072], P(('frm', 'head'))
- text_out: float32 [256, 3072], P('head')
Inputs may be any that keep to these rules, and one draw needn't show every extreme that they name: `band_start`: the window of 3 bands of every query tile contains the tile's own band.
All inputs are finite; a program needn't handle non-finite values.
Results may differ from a plain program's by a relative error of at most 0.009.
Values may be sent and summed in bfloat16 or wider, within the bound.
A program may use at most 128 MiB of HBM per device.

v0:
```python
import math

import jax
import jax.numpy as jnp
from jax import lax
from jax.sharding import PartitionSpec as P

HD = 128
TXT = 256
BANDS = 4
BAND_WIN = 3


def shifted(array, axis, by):
    length = lax.axis_size(axis)
    pairs = [(i, i + by) for i in range(length) if 0 <= i + by < length]
    return lax.ppermute(array, axis, pairs)


def combined_all(value, axis, join):
    pieces = jax.tree.map(lambda part: lax.all_gather(part, axis), value)
    head = jax.tree.map(lambda part: part[0], pieces)
    tail = jax.tree.map(lambda part: part[1:], pieces)
    subtotal, _ = lax.scan(lambda subtotal, piece: (join(subtotal, piece), None), head, tail)
    return subtotal


def merge_parts(first_part, second_part):
    top_one, total_one, mixed_one = first_part
    top_two, total_two, mixed_two = second_part
    top_both = jnp.maximum(top_one, top_two)
    factor_one = jnp.exp(top_one - top_both)
    factor_two = jnp.exp(top_two - top_both)
    total_both = total_one * factor_one + total_two * factor_two
    mixed_both = (
        mixed_one * jnp.transpose(factor_one)[:, :, None]
        + mixed_two * jnp.transpose(factor_two)[:, :, None]
    )
    return (top_both, total_both, mixed_both)


def partial_block(queries, key_block, value_block, live_keys):
    scores = jnp.einsum("qhd,khd->hqk", queries, key_block, preferred_element_type=jnp.float32)
    scores = scores * (1.0 / math.sqrt(queries.shape[2]))
    scores = jnp.where(live_keys[None, None, :], scores, -jnp.inf)
    top_raw = jnp.max(scores, axis=-1)
    top_safe = jnp.where(jnp.isfinite(top_raw), top_raw, 0.0)
    weights = jnp.exp(scores - top_safe[:, :, None])
    total_sum = jnp.sum(weights, axis=-1)
    mixed_sum = jnp.einsum(
        "hqk,khd->qhd",
        weights.astype(jnp.bfloat16),
        value_block,
        preferred_element_type=jnp.float32,
    )
    return (top_raw, total_sum, mixed_sum)


def finish_rows(running):
    top_raw, total_sum, mixed_sum = running
    return mixed_sum / jnp.transpose(total_sum)[:, :, None]


def body(
    video_q, video_k, video_v, text_q, text_k, text_v, band_start, text_mask, video_proj, text_proj
):
    tile_rows, lane_width = video_q.shape
    head_count = lane_width // HD

    def split_heads(array):
        return array.reshape(array.shape[0], head_count, HD)

    devices = lax.axis_size("frm")
    head_devices = lax.axis_size("head")
    position = lax.axis_index("frm")
    frame_count = devices // BANDS
    own_frame = position // BANDS
    first_band = band_start[0]
    text_live = text_mask == 1
    queries = split_heads(video_q)
    video_keys = split_heads(video_k)
    video_values = split_heads(video_v)
    text_keys = split_heads(text_k)
    text_values = split_heads(text_v)
    running = partial_block(queries, video_keys, video_values, jnp.ones((tile_rows,), bool))
    running = merge_parts(running, partial_block(queries, text_keys, text_values, text_live))
    offsets = sorted(
        {
            step_frame * BANDS + step_band
            for step_frame in (-1, 0, 1)
            for step_band in range(1 - BAND_WIN, BAND_WIN)
        }
        - {0}
    )
    for offset in offsets:
        moved_keys, moved_values = shifted((video_k, video_v), "frm", offset)
        source = position - offset
        source_frame = source // BANDS
        source_band = source % BANDS
        frame_fits = (
            (source_frame >= 0)
            & (source_frame < frame_count)
            & (jnp.abs(source_frame - own_frame) <= 1)
        )
        band_fits = (source_band >= first_band) & (source_band < first_band + BAND_WIN)
        usable = (source >= 0) & (source < devices) & (frame_fits & band_fits)
        live_keys = jnp.broadcast_to(usable, (tile_rows,))
        running = merge_parts(
            running,
            partial_block(queries, split_heads(moved_keys), split_heads(moved_values), live_keys),
        )
    video_attn = finish_rows(running).reshape(tile_rows, lane_width).astype(jnp.bfloat16)
    picked = lax.slice_in_dim(
        video_attn, 0, tile_rows // head_devices * lax.axis_size("head"), axis=0
    )
    video_out = lax.psum_scatter(
        jnp.dot(picked, video_proj, preferred_element_type=jnp.float32),
        "head",
        scatter_dimension=0,
        tiled=True,
    )
    text_queries = split_heads(text_q)
    local_part = partial_block(text_queries, video_keys, video_values, jnp.ones((tile_rows,), bool))
    merged = combined_all(local_part, "frm", merge_parts)
    text_part = partial_block(text_queries, text_keys, text_values, text_live)
    text_attn = (
        finish_rows(merge_parts(merged, text_part)).reshape(TXT, lane_width).astype(jnp.bfloat16)
    )
    picked = lax.slice_in_dim(text_attn, 0, TXT // head_devices * lax.axis_size("head"), axis=0)
    text_out = lax.psum_scatter(
        jnp.dot(picked, text_proj, preferred_element_type=jnp.float32),
        "head",
        scatter_dimension=0,
        tiled=True,
    )
    return (video_out, text_out)


def solution(mesh):
    return jax.shard_map(
        body,
        mesh=mesh,
        in_specs=(
            P("frm", "head"),
            P("frm", "head"),
            P("frm", "head"),
            P(None, "head"),
            P(None, "head"),
            P(None, "head"),
            P("frm"),
            P(),
            P("head", None),
            P("head", None),
        ),
        out_specs=(P(("frm", "head"), None), P("head", None)),
        check_vma=False,
    )
```

profile of v0, /device:TPU:1, one launch (start us, length us, event | category | flops | bytes accessed | tf_op | source)
XLA Modules:
  0.0 492.5 jit_solution(4135867688389616606)
XLA Ops:
  10.7 1.7 copy.159
  12.4 2.0 convolution_bitcast_fusion.15
  14.5 6.5 %collective-permute-start.20 = (bf16[256,384]{0,1:T(8,128)(2,1)S(1)}, bf16[256,384]{0,1:T(8,128)(2,1)}, u32[]{:S(2)}, u32[]{:S(2)}) collective-permute-start(bf16[256,384]{0,1:T(8,128)(2,1)S(1)} %copy.156), channel_id=1, source_target_pairs={{0,40},{8,48},{16,56},{24,64},{32,72},{40,80},{48,88},{56,96},{64,... | collective-permute-start | bytes 589832 | tf_op jit(solution)/shard_map/ppermute | solution.py:17
  21.0 5.2 %collective-permute-start.18 = (bf16[256,384]{0,1:T(8,128)(2,1)S(1)}, bf16[256,384]{0,1:T(8,128)(2,1)}, u32[]{:S(2)}, u32[]{:S(2)}) collective-permute-start(bf16[256,384]{0,1:T(8,128)(2,1)S(1)} %copy.156), channel_id=1, source_target_pairs={{0,32},{8,40},{16,48},{24,56},{32,64},{40,72},{48,80},{56,88},{64,... | collective-permute-start | bytes 589832 | tf_op jit(solution)/shard_map/ppermute | solution.py:17
  26.1 4.6 collective-permute-start.16
  30.8 2.2 collective-permute-start.14
  33.0 1.3 collective-permute-start.2
  34.6 64.6 %all-gather.4 = f32[32,3,256]{2,1,0:T(4,128)S(1)} all-gather(f32[1,3,256]{2,1,0:T(4,128)S(1)} %bitcast.579), channel_id=3, replica_groups=mesh['frm'=32,'head'=8] {'frm'}, dimensions={0}, use_global_device_ids=true | all-gather | bytes 101376 | tf_op jit(solution)/shard_map/all_gather | solution.py:21
  99.2 47.1 %all-gather.3 = f32[32,3,256]{2,1,0:T(4,128)S(1)} all-gather(f32[1,3,256]{2,1,0:T(4,128)S(1)} %bitcast.578), channel_id=2, replica_groups=mesh['frm'=32,'head'=8] {'frm'}, dimensions={0}, use_global_device_ids=true | all-gather | bytes 101376 | tf_op jit(solution)/shard_map/all_gather | solution.py:21
  146.3 1.8 copy.161
  149.2 1.4 fusion.202
  155.6 1.7 copy.164
  158.5 2.0 fusion.65
  160.4 1.3 collective-permute-start
  163.6 6.3 %collective-permute-done = bf16[256,384]{0,1:T(8,128)(2,1)S(1)} collective-permute-done((bf16[256,384]{0,1:T(8,128)(2,1)S(1)}, bf16[256,384]{0,1:T(8,128)(2,1)S(1)}, u32[]{:S(2)}, u32[]{:S(2)}) %collective-permute-start) | collective-permute-done | bytes 196640 | tf_op jit(solution)/shard_map/ppermute | solution.py:17
  169.9 1.3 collective-permute-start.6
  171.5 7.0 %collective-permute-done.6 = bf16[256,384]{0,1:T(8,128)(2,1)S(1)} collective-permute-done((bf16[256,384]{0,1:T(8,128)(2,1)S(1)}, bf16[256,384]{0,1:T(8,128)(2,1)S(1)}, u32[]{:S(2)}, u32[]{:S(2)}) %collective-permute-start.6) | collective-permute-done | bytes 196640 | tf_op jit(solution)/shard_map/ppermute | solution.py:17
  178.5 1.3 collective-permute-start.4
  180.2 13.0 %collective-permute-done.4 = bf16[256,384]{0,1:T(8,128)(2,1)S(1)} collective-permute-done((bf16[256,384]{0,1:T(8,128)(2,1)S(1)}, bf16[256,384]{0,1:T(8,128)(2,1)S(1)}, u32[]{:S(2)}, u32[]{:S(2)}) %collective-permute-start.4) | collective-permute-done | bytes 196640 | tf_op jit(solution)/shard_map/ppermute | solution.py:17
  193.2 1.9 collective-permute-start.10
  195.5 8.9 %collective-permute-done.10 = bf16[256,384]{0,1:T(8,128)(2,1)S(1)} collective-permute-done((bf16[256,384]{0,1:T(8,128)(2,1)S(1)}, bf16[256,384]{0,1:T(8,128)(2,1)S(1)}, u32[]{:S(2)}, u32[]{:S(2)}) %collective-permute-start.10) | collective-permute-done | bytes 196640 | tf_op jit(solution)/shard_map/ppermute | solution.py:17
  204.4 1.3 collective-permute-start.8
  206.6 5.0 %collective-permute-done.8 = bf16[256,384]{0,1:T(8,128)(2,1)S(1)} collective-permute-done((bf16[256,384]{0,1:T(8,128)(2,1)S(1)}, bf16[256,384]{0,1:T(8,128)(2,1)S(1)}, u32[]{:S(2)}, u32[]{:S(2)}) %collective-permute-start.8) | collective-permute-done | bytes 196640 | tf_op jit(solution)/shard_map/ppermute | solution.py:17
  211.6 2.1 collective-permute-start.12
  214.1 1.3 collective-permute-start.3
  216.7 1.3 collective-permute-start.5
  218.4 1.3 collective-permute-start.7
  219.7 2.1 fusion.190
  222.4 1.3 collective-permute-start.9
  223.7 2.1 fusion.191
  226.5 2.2 collective-permute-start.11
  228.7 2.1 fusion.189
  231.4 4.7 collective-permute-done.3
  236.1 1.9 collective-permute-start.13
  238.1 5.0 %collective-permute-start.15 = (bf16[256,384]{1,0:T(8,128)(2,1)}, bf16[256,384]{1,0:T(8,128)(2,1)S(1)}, u32[]{:S(2)}, u32[]{:S(2)}) collective-permute-start(bf16[256,384]{1,0:T(8,128)(2,1)} %param.14), channel_id=1, source_target_pairs={{0,16},{8,24},{16,32},{24,40},{32,48},{40,56},{48,64},{56,72},{64,... | collective-permute-start | bytes 589832 | tf_op jit(solution)/shard_map/ppermute | solution.py:17
  243.9 12.0 %collective-permute-start.17 = (bf16[256,384]{1,0:T(8,128)(2,1)}, bf16[256,384]{1,0:T(8,128)(2,1)S(1)}, u32[]{:S(2)}, u32[]{:S(2)}) collective-permute-start(bf16[256,384]{1,0:T(8,128)(2,1)} %param.14), channel_id=1, source_target_pairs={{0,24},{8,32},{16,40},{24,48},{32,56},{40,64},{48,72},{56,80},{64,... | collective-permute-start | bytes 589832 | tf_op jit(solution)/shard_map/ppermute | solution.py:17
  256.8 5.4 %collective-permute-start.19 = (bf16[256,384]{1,0:T(8,128)(2,1)}, bf16[256,384]{1,0:T(8,128)(2,1)}, u32[]{:S(2)}, u32[]{:S(2)}) collective-permute-start(bf16[256,384]{1,0:T(8,128)(2,1)} %param.14), channel_id=1, source_target_pairs={{0,32},{8,40},{16,48},{24,56},{32,64},{40,72},{48,80},{56,88},{64,... | collective-permute-start | bytes 589832 | tf_op jit(solution)/shard_map/ppermute | solution.py:17
  262.2 17.6 %collective-permute-start.21 = (bf16[256,384]{1,0:T(8,128)(2,1)}, bf16[256,384]{1,0:T(8,128)(2,1)}, u32[]{:S(2)}, u32[]{:S(2)}) collective-permute-start(bf16[256,384]{1,0:T(8,128)(2,1)} %param.14), channel_id=1, source_target_pairs={{0,40},{8,48},{16,56},{24,64},{32,72},{40,80},{48,88},{56,96},{64,... | collective-permute-start | bytes 589832 | tf_op jit(solution)/shard_map/ppermute | solution.py:17
  279.8 3.0 collective-permute-start.23
  282.8 1.3 collective-permute-start.1
  285.0 6.4 %collective-permute-start.22 = (bf16[256,384]{0,1:T(8,128)(2,1)S(1)}, bf16[256,384]{0,1:T(8,128)(2,1)}, u32[]{:S(2)}, u32[]{:S(2)}) collective-permute-start(bf16[256,384]{0,1:T(8,128)(2,1)S(1)} %copy.156), channel_id=1, source_target_pairs={{0,48},{8,56},{16,64},{24,72},{32,80},{40,88},{48,96},{56,104},{64... | collective-permute-start | bytes 589832 | tf_op jit(solution)/shard_map/ppermute | solution.py:17
  292.2 1.7 copy.174
  294.0 1.8 copy.179
  295.7 1.8 copy.184
  297.5 1.8 copy.189
  299.2 1.7 copy.194
  301.0 1.7 copy.199
  302.7 1.7 copy.204
  304.4 1.7 copy.209
  306.2 1.8 copy.214
  307.9 1.7 copy.219
  309.7 1.7 copy.224
  311.4 1.7 copy.169
  313.4 1.7 fusion.85
  315.2 1.3 fusion.188
  322.7 2.6 fusion.204
  326.8 9.7 %slice.39 = f32[7936,3,128]{2,0,1:T(8,128)} slice(f32[8192,3,128]{2,0,1:T(8,128)} %all-gather.7.cloned.1.call-done), slice={[256:8192], [0:3], [0:128]} | slice | bytes 24379392 | tf_op jit(solution)/shard_map/slice | solution.py:23
  336.5 82.6 %while.14 = (s32[]{:T(128)}, f32[3,256]{1,0:T(4,128)S(1)}, f32[3,256]{1,0:T(4,128)S(1)}, f32[256,3,128]{2,1,0:T(4,128)S(1)}, f32[31,3,256]{2,1,0:T(4,128)S(1)}, ...) while((s32[]{:T(128)}, f32[3,256]{1,0:T(4,128)S(1)}, f32[3,256]{1,0:T(4,128)S(1)}, ...), condition=%wide.region_32.33_spmd, body=%wide.region_31.32_spmd.sunk | while | flops 300290 | bytes 2024545 | solution.py:24
  337.9 1.3 fusion.263
  340.6 1.3 fusion.263
  343.2 1.3 fusion.263
  345.9 1.3 fusion.263
  419.7 4.4 fusion.205
  424.2 60.9 %reduce-scatter.5.cloned.1.call-done = f32[32,3072]{1,0:T(8,128)} async-done(((f32[256,3072]{1,0:T(8,128)}), f32[32,3072]{1,0:T(8,128)}) %reduce-scatter.5.cloned.1.call-update) | async-done | bytes 393232 | tf_op jit(solution)/shard_map/reduce_scatter | solution.py:130
  (518 shorter events, 103.0 us)
Async XLA Ops:
  8.0 314.7 %copy-start = (bf16[384,3072]{1,0:T(8,128)(2,1)S(1)}, bf16[384,3072]{1,0:T(8,128)(2,1)}, u32[]{:S(2)}) copy-start(bf16[384,3072]{1,0:T(8,128)(2,1)} %param.20) | copy-start | bytes 7077892
  8.0 317.4 %all-gather.7.cloned.1.call-start = ((), (), s32[]{:S(2)}) async-start(), calls=%async_computation.4 | async-start | bytes 12976128 | tf_op jit(solution)/shard_map/all_gather | solution.py:21
  10.3 88.8 %copy-start.24 = (bf16[256,384]{0,1:T(8,128)(2,1)}, bf16[256,384]{0,1:T(8,128)(2,1)S(1)}, u32[]{:S(2)}) copy-start(bf16[256,384]{0,1:T(8,128)(2,1)S(1)} %copy.226) | copy-start | bytes 589828
  10.7 138.4 %copy-start.106 = (s32[256]{0:T(256)S(1)}, s32[256]{0:T(256)}, u32[]{:S(2)}) copy-start(s32[256]{0:T(256)} %param.19) | copy-start | bytes 3076
  14.5 409.7 %reduce-scatter.3.cloned.1.call-start = ((), (), s32[]{:S(2)}) async-start(), calls=%async_computation.2 | async-start | bytes 3538944 | tf_op jit(solution)/shard_map/reduce_scatter | solution.py:116
  14.5 211.9 %collective-permute-start.20 = (bf16[256,384]{0,1:T(8,128)(2,1)S(1)}, bf16[256,384]{0,1:T(8,128)(2,1)}, u32[]{:S(2)}, u32[]{:S(2)}) collective-permute-start(bf16[256,384]{0,1:T(8,128)(2,1)S(1)} %copy.156), channel_id=1, source_target_pairs={{0,40},{8,48},{16,56},{24,64},{32,72},{40,80},{48,88},{56,96},{64,... | collective-permute-start | bytes 589832 | tf_op jit(solution)/shard_map/ppermute | solution.py:17
  21.0 197.4 %collective-permute-start.18 = (bf16[256,384]{0,1:T(8,128)(2,1)S(1)}, bf16[256,384]{0,1:T(8,128)(2,1)}, u32[]{:S(2)}, u32[]{:S(2)}) collective-permute-start(bf16[256,384]{0,1:T(8,128)(2,1)S(1)} %copy.156), channel_id=1, source_target_pairs={{0,32},{8,40},{16,48},{24,56},{32,64},{40,72},{48,80},{56,88},{64,... | collective-permute-start | bytes 589832 | tf_op jit(solution)/shard_map/ppermute | solution.py:17
  26.1 196.3 %collective-permute-start.16 = (bf16[256,384]{0,1:T(8,128)(2,1)S(1)}, bf16[256,384]{0,1:T(8,128)(2,1)}, u32[]{:S(2)}, u32[]{:S(2)}) collective-permute-start(bf16[256,384]{0,1:T(8,128)(2,1)S(1)} %copy.156), channel_id=1, source_target_pairs={{0,24},{8,32},{16,40},{24,48},{32,56},{40,64},{48,72},{56,80},{64,... | collective-permute-start | bytes 589832 | tf_op jit(solution)/shard_map/ppermute | solution.py:17
  30.8 183.3 %collective-permute-start.14 = (bf16[256,384]{0,1:T(8,128)(2,1)S(1)}, bf16[256,384]{0,1:T(8,128)(2,1)}, u32[]{:S(2)}, u32[]{:S(2)}) collective-permute-start(bf16[256,384]{0,1:T(8,128)(2,1)S(1)} %copy.156), channel_id=1, source_target_pairs={{0,16},{8,24},{16,32},{24,40},{32,48},{40,56},{48,64},{56,72},{64,... | collective-permute-start | bytes 589832 | tf_op jit(solution)/shard_map/ppermute | solution.py:17
  33.0 127.4 %collective-permute-start.2 = (bf16[256,384]{0,1:T(8,128)(2,1)S(1)}, bf16[256,384]{0,1:T(8,128)(2,1)}, u32[]{:S(2)}, u32[]{:S(2)}) collective-permute-start(bf16[256,384]{0,1:T(8,128)(2,1)S(1)} %copy.156), channel_id=1, source_target_pairs={{40,0},{48,8},{56,16},{64,24},{72,32},{80,40},{88,48},{96,56},{104... | collective-permute-start | bytes 589832 | tf_op jit(solution)/shard_map/ppermute | solution.py:17
  99.2 50.0 %copy-start.40 = (f32[32,3,256]{2,1,0:T(4,128)}, f32[32,3,256]{2,1,0:T(4,128)S(1)}, u32[]{:S(2)}) copy-start(f32[32,3,256]{2,1,0:T(4,128)S(1)} %all-gather.4) | copy-start | bytes 294916
  160.4 9.4 %collective-permute-start = (bf16[256,384]{0,1:T(8,128)(2,1)S(1)}, bf16[256,384]{0,1:T(8,128)(2,1)S(1)}, u32[]{:S(2)}, u32[]{:S(2)}) collective-permute-start(bf16[256,384]{0,1:T(8,128)(2,1)S(1)} %copy.156), channel_id=1, source_target_pairs={{48,0},{56,8},{64,16},{72,24},{80,32},{88,40},{96,48},{104,56},{11... | collective-permute-start | bytes 589832 | tf_op jit(solution)/shard_map/ppermute | solution.py:17
  163.0 80.1 %copy-start.3 = (f32[3,256,256]{1,2,0:T(8,128)}, f32[3,256,256]{1,2,0:T(8,128)S(1)}, u32[]{:S(2)}) copy-start(f32[3,256,256]{1,2,0:T(8,128)S(1)} %get-tuple-element.140) | copy-start | bytes 2359300
  163.6 79.5 %copy-start.72 = (f32[3,256]{1,0:T(4,128)}, f32[3,256]{1,0:T(4,128)S(1)}, u32[]{:S(2)}) copy-start(f32[3,256]{1,0:T(4,128)S(1)} %is-finite_select_fusion.12) | copy-start | bytes 9220
  169.9 8.7 %collective-permute-start.6 = (bf16[256,384]{0,1:T(8,128)(2,1)S(1)}, bf16[256,384]{0,1:T(8,128)(2,1)S(1)}, u32[]{:S(2)}, u32[]{:S(2)}) collective-permute-start(bf16[256,384]{0,1:T(8,128)(2,1)S(1)} %copy.156), channel_id=1, source_target_pairs={{24,0},{32,8},{40,16},{48,24},{56,32},{64,40},{72,48},{80,56},{88,... | collective-permute-start | bytes 589832 | tf_op jit(solution)/shard_map/ppermute | solution.py:17
  171.5 24.0 %copy-start.50 = (f32[3,256]{1,0:T(4,128)}, f32[3,256]{1,0:T(4,128)S(1)}, u32[]{:S(2)}) copy-start(f32[3,256]{1,0:T(4,128)S(1)} %get-tuple-element.141) | copy-start | bytes 9220
  171.5 71.6 %copy-start.20 = (f32[3,256,256]{1,2,0:T(8,128)}, f32[3,256,256]{1,2,0:T(8,128)S(1)}, u32[]{:S(2)}) copy-start(f32[3,256,256]{1,2,0:T(8,128)S(1)} %get-tuple-element.142) | copy-start | bytes 2359300
  171.5 71.6 %copy-start.91 = (f32[3,256]{1,0:T(4,128)}, f32[3,256]{1,0:T(4,128)S(1)}, u32[]{:S(2)}) copy-start(f32[3,256]{1,0:T(4,128)S(1)} %is-finite_select_fusion.13) | copy-start | bytes 9220
  178.5 14.7 %collective-permute-start.4 = (bf16[256,384]{0,1:T(8,128)(2,1)S(1)}, bf16[256,384]{0,1:T(8,128)(2,1)S(1)}, u32[]{:S(2)}, u32[]{:S(2)}) collective-permute-start(bf16[256,384]{0,1:T(8,128)(2,1)S(1)} %copy.156), channel_id=1, source_target_pairs={{32,0},{40,8},{48,16},{56,24},{64,32},{72,40},{80,48},{88,56},{96,... | collective-permute-start | bytes 589832 | tf_op jit(solution)/shard_map/ppermute | solution.py:17
  180.2 15.3 %copy-start.52 = (f32[3,256]{1,0:T(4,128)}, f32[3,256]{1,0:T(4,128)S(1)}, u32[]{:S(2)}) copy-start(f32[3,256]{1,0:T(4,128)S(1)} %get-tuple-element.135) | copy-start | bytes 9220
  180.2 75.8 %copy-start.5 = (f32[3,256,256]{1,2,0:T(8,128)}, f32[3,256,256]{1,2,0:T(8,128)S(1)}, u32[]{:S(2)}) copy-start(f32[3,256,256]{1,2,0:T(8,128)S(1)} %get-tuple-element.136) | copy-start | bytes 2359300
  180.2 75.8 %copy-start.74 = (f32[3,256]{1,0:T(4,128)}, f32[3,256]{1,0:T(4,128)S(1)}, u32[]{:S(2)}) copy-start(f32[3,256]{1,0:T(4,128)S(1)} %is-finite_select_fusion.10) | copy-start | bytes 9220
  193.2 11.2 %collective-permute-start.10 = (bf16[256,384]{0,1:T(8,128)(2,1)S(1)}, bf16[256,384]{0,1:T(8,128)(2,1)S(1)}, u32[]{:S(2)}, u32[]{:S(2)}) collective-permute-start(bf16[256,384]{0,1:T(8,128)(2,1)S(1)} %copy.156), channel_id=1, source_target_pairs={{8,0},{16,8},{24,16},{32,24},{40,32},{48,40},{56,48},{64,56},{72,6... | collective-permute-start | bytes 589832 | tf_op jit(solution)/shard_map/ppermute | solution.py:17
  195.4 10.3 %copy-start.54 = (f32[3,256]{1,0:T(4,128)}, f32[3,256]{1,0:T(4,128)S(1)}, u32[]{:S(2)}) copy-start(f32[3,256]{1,0:T(4,128)S(1)} %get-tuple-element.137) | copy-start | bytes 9220
  195.5 60.5 %copy-start.9 = (f32[3,256,256]{1,2,0:T(8,128)}, f32[3,256,256]{1,2,0:T(8,128)S(1)}, u32[]{:S(2)}) copy-start(f32[3,256,256]{1,2,0:T(8,128)S(1)} %get-tuple-element.138) | copy-start | bytes 2359300
  195.5 60.5 %copy-start.78 = (f32[3,256]{1,0:T(4,128)}, f32[3,256]{1,0:T(4,128)S(1)}, u32[]{:S(2)}) copy-start(f32[3,256]{1,0:T(4,128)S(1)} %is-finite_select_fusion.11) | copy-start | bytes 9220
  204.4 7.2 %collective-permute-start.8 = (bf16[256,384]{0,1:T(8,128)(2,1)S(1)}, bf16[256,384]{0,1:T(8,128)(2,1)S(1)}, u32[]{:S(2)}, u32[]{:S(2)}) collective-permute-start(bf16[256,384]{0,1:T(8,128)(2,1)S(1)} %copy.156), channel_id=1, source_target_pairs={{16,0},{24,8},{32,16},{40,24},{48,32},{56,40},{64,48},{72,56},{80,... | collective-permute-start | bytes 589832 | tf_op jit(solution)/shard_map/ppermute | solution.py:17
  206.1 78.0 %copy-start.7 = (f32[3,256,256]{1,2,0:T(8,128)}, f32[3,256,256]{1,2,0:T(8,128)S(1)}, u32[]{:S(2)}) copy-start(f32[3,256,256]{1,2,0:T(8,128)S(1)} %get-tuple-element.132) | copy-start | bytes 2359300
  206.6 77.4 %copy-start.76 = (f32[3,256]{1,0:T(4,128)}, f32[3,256]{1,0:T(4,128)S(1)}, u32[]{:S(2)}) copy-start(f32[3,256]{1,0:T(4,128)S(1)} %is-finite_select_fusion.8) | copy-start | bytes 9220
  211.6 5.1 %collective-permute-start.12 = (bf16[256,384]{0,1:T(8,128)(2,1)S(1)}, bf16[256,384]{0,1:T(8,128)(2,1)S(1)}, u32[]{:S(2)}, u32[]{:S(2)}) collective-permute-start(bf16[256,384]{0,1:T(8,128)(2,1)S(1)} %copy.156), channel_id=1, source_target_pairs={{0,8},{8,16},{16,24},{24,32},{32,40},{40,48},{48,56},{56,64},{64,7... | collective-permute-start | bytes 589832 | tf_op jit(solution)/shard_map/ppermute | solution.py:17
  214.0 11.8 %copy-start.58 = (f32[3,256]{1,0:T(4,128)}, f32[3,256]{1,0:T(4,128)S(1)}, u32[]{:S(2)}) copy-start(f32[3,256]{1,0:T(4,128)S(1)} %get-tuple-element.133) | copy-start | bytes 9220
  214.1 70.0 %copy-start.13 = (f32[3,256,256]{1,2,0:T(8,128)}, f32[3,256,256]{1,2,0:T(8,128)S(1)}, u32[]{:S(2)}) copy-start(f32[3,256,256]{1,2,0:T(8,128)S(1)} %get-tuple-element.134) | copy-start | bytes 2359300
  214.1 70.0 %copy-start.82 = (f32[3,256]{1,0:T(4,128)}, f32[3,256]{1,0:T(4,128)S(1)}, u32[]{:S(2)}) copy-start(f32[3,256]{1,0:T(4,128)S(1)} %is-finite_select_fusion.9) | copy-start | bytes 9220
  214.1 22.0 %collective-permute-start.3 = (bf16[256,384]{1,0:T(8,128)(2,1)}, bf16[256,384]{1,0:T(8,128)(2,1)}, u32[]{:S(2)}, u32[]{:S(2)}) collective-permute-start(bf16[256,384]{1,0:T(8,128)(2,1)} %param.14), channel_id=1, source_target_pairs={{40,0},{48,8},{56,16},{64,24},{72,32},{80,40},{88,48},{96,56},{104... | collective-permute-start | bytes 589832 | tf_op jit(solution)/shard_map/ppermute | solution.py:17
  216.7 74.7 %copy-start.11 = (f32[3,256,256]{1,2,0:T(8,128)}, f32[3,256,256]{1,2,0:T(8,128)S(1)}, u32[]{:S(2)}) copy-start(f32[3,256,256]{1,2,0:T(8,128)S(1)} %get-tuple-element.128) | copy-start | bytes 2359300
  216.7 74.7 %copy-start.80 = (f32[3,256]{1,0:T(4,128)}, f32[3,256]{1,0:T(4,128)S(1)}, u32[]{:S(2)}) copy-start(f32[3,256]{1,0:T(4,128)S(1)} %is-finite_select_fusion.6) | copy-start | bytes 9220
  216.7 21.3 %collective-permute-start.5 = (bf16[256,384]{1,0:T(8,128)(2,1)}, bf16[256,384]{1,0:T(8,128)(2,1)}, u32[]{:S(2)}, u32[]{:S(2)}) collective-permute-start(bf16[256,384]{1,0:T(8,128)(2,1)} %param.14), channel_id=1, source_target_pairs={{32,0},{40,8},{48,16},{56,24},{64,32},{72,40},{80,48},{88,56},{96,... | collective-permute-start | bytes 589832 | tf_op jit(solution)/shard_map/ppermute | solution.py:17
  218.3 19.7 %copy-start.62 = (f32[3,256]{1,0:T(4,128)}, f32[3,256]{1,0:T(4,128)S(1)}, u32[]{:S(2)}) copy-start(f32[3,256]{1,0:T(4,128)S(1)} %get-tuple-element.129) | copy-start | bytes 9220
  218.4 73.0 %copy-start.16 = (f32[3,256,256]{1,2,0:T(8,128)}, f32[3,256,256]{1,2,0:T(8,128)S(1)}, u32[]{:S(2)}) copy-start(f32[3,256,256]{1,2,0:T(8,128)S(1)} %get-tuple-element.130) | copy-start | bytes 2359300
  218.4 73.0 %copy-start.85 = (f32[3,256]{1,0:T(4,128)}, f32[3,256]{1,0:T(4,128)S(1)}, u32[]{:S(2)}) copy-start(f32[3,256]{1,0:T(4,128)S(1)} %is-finite_select_fusion.7) | copy-start | bytes 9220
  218.4 25.5 %collective-permute-start.7 = (bf16[256,384]{1,0:T(8,128)(2,1)}, bf16[256,384]{1,0:T(8,128)(2,1)S(1)}, u32[]{:S(2)}, u32[]{:S(2)}) collective-permute-start(bf16[256,384]{1,0:T(8,128)(2,1)} %param.14), channel_id=1, source_target_pairs={{24,0},{32,8},{40,16},{48,24},{56,32},{64,40},{72,48},{80,56},{88,... | collective-permute-start | bytes 589832 | tf_op jit(solution)/shard_map/ppermute | solution.py:17
  221.8 16.2 %copy-start.64 = (f32[3,256]{1,0:T(4,128)}, f32[3,256]{1,0:T(4,128)S(1)}, u32[]{:S(2)}) copy-start(f32[3,256]{1,0:T(4,128)S(1)} %get-tuple-element.123) | copy-start | bytes 9220
  222.4 34.4 %collective-permute-start.9 = (bf16[256,384]{1,0:T(8,128)(2,1)}, bf16[256,384]{1,0:T(8,128)(2,1)S(1)}, u32[]{:S(2)}, u32[]{:S(2)}) collective-permute-start(bf16[256,384]{1,0:T(8,128)(2,1)} %param.14), channel_id=1, source_target_pairs={{16,0},{24,8},{32,16},{40,24},{48,32},{56,40},{64,48},{72,56},{80,... | collective-permute-start | bytes 589832 | tf_op jit(solution)/shard_map/ppermute | solution.py:17
  225.9 17.2 %copy-start.66 = (f32[3,256]{1,0:T(4,128)}, f32[3,256]{1,0:T(4,128)S(1)}, u32[]{:S(2)}) copy-start(f32[3,256]{1,0:T(4,128)S(1)} %get-tuple-element.125) | copy-start | bytes 9220
  226.5 35.8 %collective-permute-start.11 = (bf16[256,384]{1,0:T(8,128)(2,1)}, bf16[256,384]{1,0:T(8,128)(2,1)S(1)}, u32[]{:S(2)}, u32[]{:S(2)}) collective-permute-start(bf16[256,384]{1,0:T(8,128)(2,1)} %param.14), channel_id=1, source_target_pairs={{8,0},{16,8},{24,16},{32,24},{40,32},{48,40},{56,48},{64,56},{72,6... | collective-permute-start | bytes 589832 | tf_op jit(solution)/shard_map/ppermute | solution.py:17
  230.8 12.2 %copy-start.68 = (f32[3,256]{1,0:T(4,128)}, f32[3,256]{1,0:T(4,128)S(1)}, u32[]{:S(2)}) copy-start(f32[3,256]{1,0:T(4,128)S(1)} %get-tuple-element.121) | copy-start | bytes 9220
  236.1 43.7 %collective-permute-start.13 = (bf16[256,384]{1,0:T(8,128)(2,1)}, bf16[256,384]{1,0:T(8,128)(2,1)S(1)}, u32[]{:S(2)}, u32[]{:S(2)}) collective-permute-start(bf16[256,384]{1,0:T(8,128)(2,1)} %param.14), channel_id=1, source_target_pairs={{0,8},{8,16},{16,24},{24,32},{32,40},{40,48},{48,56},{56,64},{64,7... | collective-permute-start | bytes 589832 | tf_op jit(solution)/shard_map/ppermute | solution.py:17
  238.1 44.7 %collective-permute-start.15 = (bf16[256,384]{1,0:T(8,128)(2,1)}, bf16[256,384]{1,0:T(8,128)(2,1)S(1)}, u32[]{:S(2)}, u32[]{:S(2)}) collective-permute-start(bf16[256,384]{1,0:T(8,128)(2,1)} %param.14), channel_id=1, source_target_pairs={{0,16},{8,24},{16,32},{24,40},{32,48},{40,56},{48,64},{56,72},{64,... | collective-permute-start | bytes 589832 | tf_op jit(solution)/shard_map/ppermute | solution.py:17
  243.9 47.5 %copy-start.42 = (bf16[256,384]{1,0:T(8,128)(2,1)}, bf16[256,384]{1,0:T(8,128)(2,1)S(1)}, u32[]{:S(2)}) copy-start(bf16[256,384]{1,0:T(8,128)(2,1)S(1)} %collective-permute-done.7) | copy-start | bytes 589828
  243.9 41.1 %collective-permute-start.17 = (bf16[256,384]{1,0:T(8,128)(2,1)}, bf16[256,384]{1,0:T(8,128)(2,1)S(1)}, u32[]{:S(2)}, u32[]{:S(2)}) collective-permute-start(bf16[256,384]{1,0:T(8,128)(2,1)} %param.14), channel_id=1, source_target_pairs={{0,24},{8,32},{16,40},{24,48},{32,56},{40,64},{48,72},{56,80},{64,... | collective-permute-start | bytes 589832 | tf_op jit(solution)/shard_map/ppermute | solution.py:17
  256.8 34.5 %copy-start.43 = (bf16[256,384]{1,0:T(8,128)(2,1)}, bf16[256,384]{1,0:T(8,128)(2,1)S(1)}, u32[]{:S(2)}) copy-start(bf16[256,384]{1,0:T(8,128)(2,1)S(1)} %collective-permute-done.9) | copy-start | bytes 589828
  256.8 49.4 %collective-permute-start.19 = (bf16[256,384]{1,0:T(8,128)(2,1)}, bf16[256,384]{1,0:T(8,128)(2,1)}, u32[]{:S(2)}, u32[]{:S(2)}) collective-permute-start(bf16[256,384]{1,0:T(8,128)(2,1)} %param.14), channel_id=1, source_target_pairs={{0,32},{8,40},{16,48},{24,56},{32,64},{40,72},{48,80},{56,88},{64,... | collective-permute-start | bytes 589832 | tf_op jit(solution)/shard_map/ppermute | solution.py:17
  262.2 29.2 %copy-start.44 = (bf16[256,384]{1,0:T(8,128)(2,1)}, bf16[256,384]{1,0:T(8,128)(2,1)S(1)}, u32[]{:S(2)}) copy-start(bf16[256,384]{1,0:T(8,128)(2,1)S(1)} %collective-permute-done.11) | copy-start | bytes 589828
  262.2 45.7 %collective-permute-start.21 = (bf16[256,384]{1,0:T(8,128)(2,1)}, bf16[256,384]{1,0:T(8,128)(2,1)}, u32[]{:S(2)}, u32[]{:S(2)}) collective-permute-start(bf16[256,384]{1,0:T(8,128)(2,1)} %param.14), channel_id=1, source_target_pairs={{0,40},{8,48},{16,56},{24,64},{32,72},{40,80},{48,88},{56,96},{64,... | collective-permute-start | bytes 589832 | tf_op jit(solution)/shard_map/ppermute | solution.py:17
  279.8 11.6 %copy-start.45 = (bf16[256,384]{1,0:T(8,128)(2,1)}, bf16[256,384]{1,0:T(8,128)(2,1)S(1)}, u32[]{:S(2)}) copy-start(bf16[256,384]{1,0:T(8,128)(2,1)S(1)} %collective-permute-done.13) | copy-start | bytes 589828
  279.8 29.9 %collective-permute-start.23 = (bf16[256,384]{1,0:T(8,128)(2,1)}, bf16[256,384]{1,0:T(8,128)(2,1)}, u32[]{:S(2)}, u32[]{:S(2)}) collective-permute-start(bf16[256,384]{1,0:T(8,128)(2,1)} %param.14), channel_id=1, source_target_pairs={{0,48},{8,56},{16,64},{24,72},{32,80},{40,88},{48,96},{56,104},{64... | collective-permute-start | bytes 589832 | tf_op jit(solution)/shard_map/ppermute | solution.py:17
  282.8 28.6 %collective-permute-start.1 = (bf16[256,384]{1,0:T(8,128)(2,1)}, bf16[256,384]{1,0:T(8,128)(2,1)}, u32[]{:S(2)}, u32[]{:S(2)}) collective-permute-start(bf16[256,384]{1,0:T(8,128)(2,1)} %param.14), channel_id=1, source_target_pairs={{48,0},{56,8},{64,16},{72,24},{80,32},{88,40},{96,48},{104,56},{11... | collective-permute-start | bytes 589832 | tf_op jit(solution)/shard_map/ppermute | solution.py:17
  285.0 30.2 %collective-permute-start.22 = (bf16[256,384]{0,1:T(8,128)(2,1)S(1)}, bf16[256,384]{0,1:T(8,128)(2,1)}, u32[]{:S(2)}, u32[]{:S(2)}) collective-permute-start(bf16[256,384]{0,1:T(8,128)(2,1)S(1)} %copy.156), channel_id=1, source_target_pairs={{0,48},{8,56},{16,64},{24,72},{32,80},{40,88},{48,96},{56,104},{64... | collective-permute-start | bytes 589832 | tf_op jit(solution)/shard_map/ppermute | solution.py:17
  325.4 159.7 %reduce-scatter.5.cloned.1.call-start = ((), (), s32[]{:S(2)}) async-start(), calls=%async_computation.3 | async-start | bytes 3538944 | tf_op jit(solution)/shard_map/reduce_scatter | solution.py:130
  336.5 82.8 %copy-start.90 = (f32[3,256]{1,0:T(4,128)S(1)}, f32[3,256]{1,0:T(4,128)}, u32[]{:S(2)}) copy-start(f32[3,256]{1,0:T(4,128)} %copy-done.89) | copy-start | bytes 9220
  336.5 82.8 %copy-start.103 = (f32[3,256]{1,0:T(4,128)S(1)}, f32[3,256]{1,0:T(4,128)}, u32[]{:S(2)}) copy-start(f32[3,256]{1,0:T(4,128)} %fusion.95) | copy-start | bytes 9220
  336.5 82.9 %copy-start.23 = (f32[3,256,256]{1,2,0:T(8,128)S(1)}, f32[3,256,256]{1,2,0:T(8,128)}, u32[]{:S(2)}) copy-start(f32[3,256,256]{1,2,0:T(8,128)} %copy-done.22) | copy-start | bytes 2359300
  336.5 82.9 %copy-start.105 = (f32[3,256]{1,0:T(4,128)S(1)}, f32[3,256]{1,0:T(4,128)}, u32[]{:S(2)}) copy-start(f32[3,256]{1,0:T(4,128)} %copy-done.104) | copy-start | bytes 9220
  419.7 65.4 %copy-start.1 = (bf16[384,3072]{1,0:T(8,128)(2,1)S(1)}, bf16[384,3072]{1,0:T(8,128)(2,1)}, u32[]{:S(2)}) copy-start(bf16[384,3072]{1,0:T(8,128)(2,1)} %param.20) | copy-start | bytes 7077892
  (72 other events, 199.0 us)
Sparse Core Ops, SparseCore 0:
  14.6 115.4 all-gather.6
Sparse Core Ops, SparseCore 1:
  325.5 60.7 reduce-scatter.2
  424.2 60.8 reduce-scatter.4
where the time goes:
time: 498 us; the launch traced here: 492 us
  blocking collectives  112 us (22%)
  waiting for transfers between devices  106 us (21%)
  starting transfers between devices  88.9 us (18%)
  local copies, waits for them, and re-layouts  85.2 us (17%)
  other arithmetic  51.6 us (10%)
  matrix products  28.8 us (6%)
  between operations  18.7 us (4%)
    all_gather x2, blocking collectives, combined_all(): pieces = jax.tree.map(lambda part: lax.all_gather(part, axis), value)  112 us
    ppermute x24, starting transfers between devices, shifted(): return lax.ppermute(array, axis, pairs)  88.8 us
    reduce_scatter x1, waiting for transfers between devices, body(): lax.psum_scatter(jnp.dot(picked, text_proj, preferred_element_type=jnp.fl...  60.9 us
    ppermute x24, waiting for transfers between devices, shifted(): return lax.ppermute(array, axis, pairs)  44.9 us
    add x31, other arithmetic, merge_parts(): mixed_one * jnp.transpose(factor_one)[:, :, None]  39.1 us
    dynamic_slice x31, local copies, waits for them, and re-layouts, combined_all(): lax.scan(lambda subtotal, piece: (join(subtotal, piece), None), head, tail)  32.1 us
    ppermute x12, local copies, waits for them, and re-layouts, shifted(): return lax.ppermute(array, axis, pairs)  20.9 us
    dot_general x16, matrix products, partial_block(): jnp.einsum('qhd,khd->hqk', queries, key_block, preferred_element_type=jnp...  15.5 us
  transfers between devices with their start and end apart: 27, of which 7 were waited for; matrix products, arithmetic and copies ran while one was open for 32% of the time, Pallas kernels for 0%

commit v1 on v0

v1 whole, which is shorter than its diff:
```python
import math

import jax
import jax.numpy as jnp
from jax import lax
from jax.experimental import pallas as pl
from jax.experimental.pallas import tpu as pltpu
from jax.sharding import PartitionSpec as P

HD = 128
TXT = 256
BANDS = 4
HEADS_HERE = 3
LANES = HEADS_HERE * HD
WIDTH = 3072
MESH = pl.DeviceIdType.MESH
BF = jnp.bfloat16
F32 = jnp.float32
FACTOR = math.log2(math.e) / math.sqrt(HD)
DEAD = -1e30
CHUNKS = 2
OWN, MATE, OPP, INTER, VMATE, VERT = range(6)
Z_FIRST = ((0, 1024),)
Y_FIRST = ((1024, 1024), (2048, 1024))
BLOCK = 512


def dot_nt(a, b):
    return lax.dot_general(a, b, (((1,), (1,)), ((), ())), preferred_element_type=F32)


def dot_nn(a, b):
    return jnp.dot(a, b, preferred_element_type=F32)


def with_ones(values):
    return jnp.concatenate([values, jnp.ones(values.shape, BF)], axis=1)


def kernel(
    vq_hbm, vk_hbm, vv_hbm, tq_hbm, tk_hbm, tv_hbm, band_ref, mask_ref, vproj_hbm, tproj_hbm,
    vout_ref, tout_ref,
    kv_a, kv_b, kv_c, vq, tq, tk, tv, vproj, tproj, state_o, state_m, attn, part,
    kv_send, kv_recv, load_sem,
    t_a, t_ar, t_b, t_br, t_c, t_cr, t_z, t_zr, t_rows, t_sums, t_sumr, t_out,
    ta_sem, tz_send, tz_recv, tg_send, tg_recv, ts_send, ts_recv, to_send, to_recv,
    zf_in, zf_sum, r1, r2, stage, zs, zr,
    zf_sem, r_send, r_recv, zx_sem,
):
    frm = lax.axis_index("frm")
    head = lax.axis_index("head")
    zh, x, c = frm // 8, (frm // 2) % 4, frm % 2
    zl, y = head // 4, head % 4
    xr, xo = x // 2, x % 2

    def at(zh_, x_, c_):
        return {"frm": zh_ * 8 + x_ * 2 + c_, "head": head}

    def at_head(zl_, y_):
        return {"frm": frm, "head": zl_ * 4 + y_}

    x_mate = x + 1 - 2 * xo
    sib = at(zh, x, 1 - c)
    mate = at(zh, x_mate, c)
    inter = at(zh, 3 - x, c)
    z_pair = at_head(1 - zl, y)
    yp, ym, yo = (y + 1) % 4, (y + 3) % 4, (y + 2) % 4
    zh_to = zh + 1 - 2 * xr
    v_send = (zh_to >= 0) & (zh_to <= 3)
    zh_from = zh - 1 + 2 * xr
    v_recv = (zh_from >= 0) & (zh_from <= 3)
    vert = at(jnp.clip(zh_to, 0, 3), x, c)

    def copy_to(src, dst, send, recv, device):
        return pltpu.make_async_remote_copy(
            src_ref=src, dst_ref=dst, send_sem=send, recv_sem=recv,
            device_id=device, device_id_type=MESH,
        )

    loads = []

    def load(src, dst):
        copy = pltpu.make_async_copy(src, dst, load_sem.at[len(loads)])
        copy.start()
        loads.append(copy)
        return copy

    load_own = [load(vk_hbm, kv_a.at[0, 0]), load(vv_hbm, kv_a.at[0, 1])]
    load_text = [load(tq_hbm, tq), load(tk_hbm, tk), load(tv_hbm, tv)]
    load_q = load(vq_hbm, vq)
    load_vproj = load(vproj_hbm, vproj)
    piece = 2 * x + zh // 2
    load_tproj = load(tproj_hbm.at[:, pl.ds(pl.multiple_of(piece * LANES, LANES), LANES)], tproj)

    frm_partners = [sib]
    for dz in range(4):
        for dx in range(4):
            if (dz, dx) != (0, 0) and (dz % 2 == 0 or dx == 0):
                frm_partners.append(at((zh + dz) % 4, (x + dx) % 4, c))
    gather_partners = [
        at((zh + dz) % 4, (x + dx) % 4, c)
        for dz in (0, 2) for dx in range(4) if (dz, dx) != (0, 0)
    ]
    head_partners = [
        ((zl + dz) % 2, (y + dy) % 4) for dz in range(2) for dy in range(4) if (dz, dy) != (0, 0)
    ]
    barrier = pltpu.get_barrier_semaphore()
    for device in frm_partners + [at_head(a, b) for a, b in head_partners]:
        pl.semaphore_signal(barrier, inc=1, device_id=device, device_id_type=MESH)
    pl.semaphore_wait(barrier, len(frm_partners) + len(head_partners))

    rows = 256 // CHUNKS
    sends = []

    def kv_copy(kind, t, j, src_slot, dst_slot, device, src=None):
        rng = pl.ds(j * rows, rows)
        return copy_to(
            kv_of[src_slot // 4].at[src_slot % 4, t, rng] if src is None else src.at[rng],
            kv_of[dst_slot // 4].at[dst_slot % 4, t, rng],
            kv_send.at[kind, t, j],
            kv_recv.at[dst_slot, t, j],
            device,
        )

    kv_of = (kv_a, kv_b, kv_c)
    pieces = [(t, j) for t in range(2) for j in range(CHUNKS)]
    own_hbm = (vk_hbm, vv_hbm)

    def to_mate(t, j):
        return kv_copy(0, t, j, 0, 2 * MATE, mate, own_hbm[t])

    def to_inter(t, j):
        return kv_copy(1, t, j, 0, 2 * INTER, inter, own_hbm[t])

    def to_opp(t, j):
        if t == 0:
            return kv_copy(2, t, j, 2 * INTER, 2 * OPP, mate)
        return kv_copy(2, t, j, 2 * MATE, 2 * OPP, inter)

    def to_vert(t, j):
        return kv_copy(3, t, j, 2 * INTER, 2 * VERT, vert)

    def to_vmate(t, j):
        return kv_copy(4, t, j, 2 * VERT, 2 * VMATE, mate)

    def to_sib(role, t, j):
        return kv_copy(5 + role, t, j, 2 * role, 2 * role + 1, sib, own_hbm[t] if role == OWN else None)

    def go(copy):
        copy.start()
        sends.append(copy)

    for t, j in pieces:
        go(to_inter(t, j))
        go(to_mate(t, j))
    for t, j in pieces:
        go(to_sib(OWN, t, j))

    for copy in load_own + load_text:
        copy.wait()
    lane = lax.broadcasted_iota(jnp.int32, (1, TXT), 1)
    text_bias = jnp.where(mask_ref[...] == 1, 0.0, DEAD)
    first_bias = jnp.where(frm == 0, text_bias, DEAD)

    def pack_stats(tops, totals):
        count = tops[0].shape[0]
        at_lane = lax.broadcasted_iota(jnp.int32, (count, HD), 1)
        packed = jnp.zeros((count, HD), F32)
        for h in range(HEADS_HERE):
            high = totals[h].astype(BF).astype(F32)
            packed = jnp.where(at_lane == h, tops[h], packed)
            packed = jnp.where(at_lane == 3 + h, high, packed)
            packed = jnp.where(at_lane == 6 + h, totals[h] - high, packed)
        return packed

    tops, totals, mixed = [], [], []
    for h in range(HEADS_HERE):
        cols = slice(h * HD, (h + 1) * HD)
        s_own = dot_nt(tq[:, cols], kv_a[0, 0, :, cols])
        s_text = dot_nt(tq[:, cols], tk[:, cols]) + first_bias
        top = jnp.maximum(
            jnp.max(s_own, axis=1, keepdims=True), jnp.max(s_text, axis=1, keepdims=True)
        ).astype(BF).astype(F32)
        base = top * FACTOR
        w_own = jnp.exp2(s_own * FACTOR - base).astype(BF)
        w_text = jnp.exp2(s_text * FACTOR - base).astype(BF)
        both = dot_nn(w_own, with_ones(kv_a[0, 1, :, cols])) + dot_nn(w_text, with_ones(tv[:, cols]))
        tops.append(top)
        totals.append(both[:, HD:HD + 1])
        mixed.append(both[:, :HD].astype(BF))
    stats = pack_stats(tops, totals).astype(BF)
    for h_to in range(8):
        for half in range(2):
            rng = slice(32 * h_to + 16 * half, 32 * h_to + 16 * half + 16)
            for h in range(HEADS_HERE):
                t_a[half, h_to, :, h * HD:(h + 1) * HD] = mixed[h][rng]
            t_a[half, h_to, :, LANES:] = stats[rng]

    text_a = copy_to(t_a.at[1 - c], t_ar, ta_sem.at[0], ta_sem.at[1], sib)
    go(text_a)

    def merge(parts):
        parts = [p.astype(F32) for p in parts]
        out_tops, out_totals, out_mixed = [], [], []
        for h in range(HEADS_HERE):
            tops_h = [p[:, LANES + h:LANES + h + 1] for p in parts]
            top = tops_h[0]
            for other in tops_h[1:]:
                top = jnp.maximum(top, other)
            total, mix = 0.0, 0.0
            for p, top_p in zip(parts, tops_h):
                weight = jnp.exp2((top_p - top) * FACTOR)
                total_p = p[:, LANES + 3 + h:LANES + 4 + h] + p[:, LANES + 6 + h:LANES + 7 + h]
                total = total + total_p * weight
                mix = mix + p[:, h * HD:(h + 1) * HD] * weight
            out_tops.append(top)
            out_totals.append(total)
            out_mixed.append(mix)
        return out_tops, out_totals, out_mixed

    def merged(parts):
        out_tops, out_totals, out_mixed = merge(parts)
        return jnp.concatenate(out_mixed + [pack_stats(out_tops, out_totals)], axis=1)

    def group(kv, fresh):
        mid = c != xo
        at_b = jnp.where(mid, 3, 1)
        pick_same = mid & (band_ref[0] == xo)
        at_c = jnp.where(pick_same, 1, 2)
        slots = (0, at_b, at_c)

        @pl.loop(0, HEADS_HERE)
        def _(h):
            cols = pl.ds(pl.multiple_of(h * HD, HD), HD)
            query = vq[:, cols]
            scores = [dot_nt(query, kv[s, 0, :, cols]) for s in slots]
            top = jnp.max(jnp.maximum(jnp.maximum(scores[0], scores[1]), scores[2]), axis=1, keepdims=True)
            if not fresh:
                old = state_m[h]
                top = jnp.maximum(top, old[:, :1])
            base = top * FACTOR
            total = None
            for s, score in zip(slots, scores):
                weights = jnp.exp2(score * FACTOR - base).astype(BF)
                term = dot_nn(weights, with_ones(kv[s, 1, :, cols]))
                total = term if total is None else total + term
            if not fresh:
                total = total + state_o[h] * jnp.exp2(old[:, :1] * FACTOR - base)
            state_o[h] = total
            state_m[h] = jnp.broadcast_to(top, (256, HD))

    def text_keys():
        @pl.loop(0, HEADS_HERE)
        def _(h):
            cols = pl.ds(pl.multiple_of(h * HD, HD), HD)
            score = dot_nt(vq[:, cols], tk[:, cols]) + text_bias
            old = state_m[h]
            top = jnp.maximum(jnp.max(score, axis=1, keepdims=True), old[:, :1])
            base = top * FACTOR
            weights = jnp.exp2(score * FACTOR - base).astype(BF)
            total = dot_nn(weights, with_ones(tv[:, cols]))
            state_o[h] = total + state_o[h] * jnp.exp2(old[:, :1] * FACTOR - base)
            state_m[h] = jnp.broadcast_to(top, (256, HD))

    def serve(t, j):
        to_inter(t, j).wait_recv()

        @pl.when(v_send)
        def _():
            to_vert(t, j).start()

        if t == 0:
            go(to_opp(t, j))
        go(to_sib(INTER, t, j))
        to_mate(t, j).wait_recv()
        if t == 1:
            go(to_opp(t, j))
        go(to_sib(MATE, t, j))

    def text_step_a():
        text_a.wait_recv()
        for h_to in range(8):
            t_b[h_to // 4, h_to % 4] = merged([t_a[c, h_to], t_ar[h_to]]).astype(BF)
        copy = copy_to(t_b.at[1 - xr], t_br, ta_sem.at[2], ta_sem.at[3], inter)
        go(copy)
        return copy

    def text_step_b(copy):
        copy.wait_recv()
        for k in range(4):
            t_c[k // 2, k % 2] = merged([t_b[xr, k], t_br[k]]).astype(BF)
        copy = copy_to(t_c.at[1 - xo], t_cr, ta_sem.at[4], ta_sem.at[5], mate)
        go(copy)
        return copy

    def text_step_c(copy):
        copy.wait_recv()
        for k in range(2):
            both = merged([t_c[xo, k], t_cr[k]])
            t_z[2 * k] = both[:8]
            t_z[2 * k + 1] = both[8:]
        copies = []
        for dz in range(1, 4):
            to = (zh + dz) % 4
            copy = copy_to(t_z.at[to], t_zr.at[dz], tz_send.at[dz], tz_recv.at[dz], at(to, x, c))
            go(copy)
            copies.append(copy)
        return copies

    def text_step_z(copies):
        for copy in copies:
            copy.wait_recv()
        _, sums, mix = merge([t_z[zh], t_zr[1], t_zr[2], t_zr[3]])
        for h in range(HEADS_HERE):
            t_rows[piece, :, h * HD:(h + 1) * HD] = (mix[h] / sums[h]).astype(BF).astype(F32)
        out = []
        for k, device in enumerate(gather_partners):
            copy = copy_to(t_rows.at[piece], t_rows.at[piece], tg_send.at[k], tg_recv.at[k], device)
            go(copy)
            out.append(copy)
        return out

    def text_gather(copies):
        k = 0
        for dz in (0, 2):
            for dx in range(4):
                if (dz, dx) == (0, 0):
                    continue
                source = 2 * ((x - dx + 4) % 4) + ((zh - dz + 4) % 4) // 2
                copy_to(
                    t_rows.at[source], t_rows.at[source], tg_send.at[k], tg_recv.at[k], sib
                ).wait_recv()
                k += 1
        load_tproj.wait()
        rows_all = jnp.concatenate([t_rows[k] for k in range(8)], axis=0).astype(BF)
        product = dot_nn(rows_all, tproj[...])
        for k in range(8):
            t_sums[k] = product[8 * k:8 * k + 8]
        out = []
        for k, (a, b) in enumerate(head_partners):
            copy = copy_to(t_sums.at[a * 4 + b], t_sumr.at[k], ts_send.at[k], ts_recv.at[k], at_head(a, b))
            go(copy)
            out.append(copy)
        return out

    def text_sum(copies):
        for copy in copies:
            copy.wait_recv()
        total = t_sums[head]
        for k in range(7):
            total = total + t_sumr[k]
        t_out[c, zh % 2, x, zh // 2] = total
        out = []
        for dz in range(1, 4):
            block = t_out.at[c, zh % 2, x, zh // 2]
            copy = copy_to(block, block, to_send.at[dz], to_recv.at[dz], at((zh + dz) % 4, x, c))
            go(copy)
            out.append(copy)
        return out

    def text_spread_mate():
        for dz in range(1, 4):
            source = (zh - dz + 4) % 4
            block = t_out.at[c, source % 2, x, source // 2]
            copy_to(block, block, to_send.at[dz], to_recv.at[dz], sib).wait_recv()
        block = t_out.at[c, :, x]
        go(copy_to(block, block, to_send.at[4], to_recv.at[4], mate))

    def text_spread_inter():
        block = t_out.at[c, :, x_mate]
        copy_to(block, block, to_send.at[4], to_recv.at[4], mate).wait_recv()
        block = t_out.at[c, :, pl.ds(2 * xr, 2)]
        go(copy_to(block, block, to_send.at[5], to_recv.at[5], inter))

    def text_spread_sib():
        block = t_out.at[c, :, pl.ds(2 - 2 * xr, 2)]
        copy_to(block, block, to_send.at[5], to_recv.at[5], inter).wait_recv()
        go(copy_to(t_out.at[c], t_out.at[c], to_send.at[6], to_recv.at[6], sib))

    def text_finish():
        block = t_out.at[1 - c]
        copy_to(block, block, to_send.at[6], to_recv.at[6], sib).wait_recv()
        for cc in range(2):
            for q in range(2):
                for k in range(8):
                    tout_ref[16 * cc + 8 * q:16 * cc + 8 * q + 8, k * LANES:(k + 1) * LANES] = (
                        t_out[cc, q, k // 2, k % 2]
                    )

    serve(*pieces[0])
    text_copy = text_step_a()
    serve(*pieces[1])
    text_copy = text_step_b(text_copy)
    for p in pieces[2:]:
        serve(*p)
    text_copies = text_step_c(text_copy)

    load_q.wait()
    for role in (OWN, MATE):
        for t, j in pieces:
            to_sib(role, t, j).wait_recv()
    group(kv_a, True)

    text_copies = text_step_z(text_copies)

    def serve_vert(t, j):
        @pl.when(v_recv)
        def _():
            to_vert(t, j).wait_recv()
            to_vmate(t, j).start()
            to_sib(VERT, t, j).start()

    serve_vert(*pieces[0])
    for t, j in pieces:
        to_opp(t, j).wait_recv()
        go(to_sib(OPP, t, j))
    text_keys()
    serve_vert(*pieces[1])

    for role in (OPP, INTER):
        for t, j in pieces:
            to_sib(role, t, j).wait_recv()
    group(kv_b, False)
    serve_vert(*pieces[2])
    text_copies = text_gather(text_copies)

    for p in pieces[3:]:
        serve_vert(*p)

    @pl.when(v_recv)
    def _():
        for t, j in pieces:
            to_vmate(t, j).wait_recv()
            to_sib(VMATE, t, j).start()
        for role in (VERT, VMATE):
            for t, j in pieces:
                to_sib(role, t, j).wait_recv()
        group(kv_c, False)

    for h in range(HEADS_HERE):
        both = state_o[h]
        attn[:, h * HD:(h + 1) * HD] = (both[:, :HD] / both[:, HD:]).astype(BF)
    load_vproj.wait()

    def project(start, width):
        @pl.loop(0, width // BLOCK)
        def _(i):
            cols = pl.ds(pl.multiple_of(start + i * BLOCK, BLOCK), BLOCK)
            product = dot_nn(attn[...], vproj[:, cols]).astype(BF)
            for k in range(8):
                part[k // 4, k % 4, :, cols] = product[32 * k:32 * k + 32]

    zf_copies = []
    for i, (start, width) in enumerate(Z_FIRST):
        project(start, width)
        copy = copy_to(
            part.at[1 - zl, :, :, pl.ds(start, width)], zf_in.at[i], zf_sem.at[0, i], zf_sem.at[1, i], z_pair
        )
        go(copy)
        zf_copies.append(copy)

    y_next, y_prev = at_head(zl, yp), at_head(zl, ym)

    def ring_start(i, block, half):
        one = [
            copy_to(block(yo, 0), r1.at[i, 0], r_send.at[i, 0], r_recv.at[i, 0], y_next),
            copy_to(block(yo, half), r1.at[i, 1], r_send.at[i, 1], r_recv.at[i, 1], y_prev),
        ]
        plain = [
            copy_to(block(yp, half), r2.at[i, 0, 1], r_send.at[i, 2], r_recv.at[i, 2], y_next),
            copy_to(block(ym, 0), r2.at[i, 1, 0], r_send.at[i, 3], r_recv.at[i, 3], y_prev),
        ]
        for copy in one + plain:
            go(copy)
        return one, plain

    def ring_middle(i, block, half, one):
        out = []
        for d, (copy, near, device, lo) in enumerate(
            zip(one, (yp, ym), (y_next, y_prev), (0, half))
        ):
            copy.wait_recv()
            stage[i, d] = (block(near, lo)[...].astype(F32) + r1[i, d].astype(F32)).astype(BF)
            summed = copy_to(
                stage.at[i, d], r2.at[i, d, d], r_send.at[i, 4 + d], r_recv.at[i, 4 + d], device
            )
            go(summed)
            out.append(summed)
        return out

    def ring_end(i, copies, mine):
        for copy in copies:
            copy.wait_recv()
        return [
            mine(k) + r2[i, 0, k].astype(F32) + r2[i, 1, k].astype(F32) for k in range(2)
        ]

    def part_block(start, half):
        def block(y_at, lo):
            return part.at[:, y_at, :, pl.ds(start + lo, half)]
        return block

    def sum_block(half):
        def block(y_at, lo):
            return zf_sum.at[0, :, y_at, :, pl.ds(lo, half)]
        return block

    half = 512
    rings = []
    for i, (start, width) in enumerate(Y_FIRST):
        project(start, width)
        rings.append(ring_start(i, part_block(start, half), half))
    text_copies = text_sum(text_copies)
    second = []
    for i, (start, width) in enumerate(Y_FIRST):
        second.append(ring_middle(i, part_block(start, half), half, rings[i][0]))
    text_spread_mate()

    zf_copies[0].wait_recv()
    start = Z_FIRST[0][0]
    for k in range(4):
        zf_sum[0, 0, k] = (
            part[zl, k, :, start:start + 1024].astype(F32) + zf_in[0, k].astype(F32)
        ).astype(BF)

    def z_block(y_at, lo):
        return zf_sum.at[0, 0, y_at, :, pl.ds(lo, half)]

    i_z = len(Y_FIRST)
    one_z = [
        copy_to(z_block(yo, 0), r1.at[i_z, 0, 0], r_send.at[i_z, 0], r_recv.at[i_z, 0], y_next),
        copy_to(z_block(yo, half), r1.at[i_z, 1, 0], r_send.at[i_z, 1], r_recv.at[i_z, 1], y_prev),
    ]
    plain_z = [
        copy_to(z_block(yp, half), r2.at[i_z, 0, 1, 0], r_send.at[i_z, 2], r_recv.at[i_z, 2], y_next),
        copy_to(z_block(ym, 0), r2.at[i_z, 1, 0, 0], r_send.at[i_z, 3], r_recv.at[i_z, 3], y_prev),
    ]
    for copy in one_z + plain_z:
        go(copy)

    text_spread_inter()

    z_copies = []
    own_sums = []
    for i, (start, width) in enumerate(Y_FIRST):
        def mine(k, start=start):
            return part[:, y, :, start + k * half:start + (k + 1) * half].astype(F32)
        sums = ring_end(i, rings[i][1] + second[i], mine)
        for k in range(2):
            zs[i, :, :, k * half:(k + 1) * half] = sums[k].astype(BF)
            vout_ref[:, start + k * half:start + (k + 1) * half] = jnp.where(zl == 0, sums[k][0], sums[k][1])
        copy = copy_to(zs.at[i, 1 - zl], zr.at[i], zx_sem.at[0, i], zx_sem.at[1, i], z_pair)
        go(copy)
        z_copies.append(copy)

    second_z = []
    for d, (copy, near, device, lo) in enumerate(
        zip(one_z, (yp, ym), (y_next, y_prev), (0, half))
    ):
        copy.wait_recv()
        stage[i_z, d, 0] = (z_block(near, lo)[...].astype(F32) + r1[i_z, d, 0].astype(F32)).astype(BF)
        summed = copy_to(
            stage.at[i_z, d, 0], r2.at[i_z, d, d, 0], r_send.at[i_z, 4 + d], r_recv.at[i_z, 4 + d], device
        )
        go(summed)
        second_z.append(summed)
    text_spread_sib()
    for copy in plain_z + second_z:
        copy.wait_recv()
    for k in range(2):
        start = Z_FIRST[0][0] + k * half
        vout_ref[:, start:start + half] = (
            zf_sum[0, 0, y, :, k * half:(k + 1) * half].astype(F32)
            + r2[i_z, 0, k, 0].astype(F32)
            + r2[i_z, 1, k, 0].astype(F32)
        )
    for i, (start, width) in enumerate(Y_FIRST):
        z_copies[i].wait_recv()
        vout_ref[:, start:start + width] = vout_ref[:, start:start + width] + zr[i].astype(F32)
    text_finish()

    for copy in sends:
        copy.wait_send()

    @pl.when(v_send)
    def _():
        for t, j in pieces:
            to_vert(t, j).wait_send()

    @pl.when(v_recv)
    def _():
        for t, j in pieces:
            to_vmate(t, j).wait_send()
            to_sib(VERT, t, j).wait_send()
            to_sib(VMATE, t, j).wait_send()


def body(video_q, video_k, video_v, text_q, text_k, text_v, band_start, text_mask, video_proj, text_proj):
    dma = pltpu.SemaphoreType.DMA
    vmem = pltpu.VMEM
    any_spec = pl.BlockSpec(memory_space=pl.ANY)
    vmem_spec = pl.BlockSpec(memory_space=pltpu.VMEM)
    smem_spec = pl.BlockSpec(memory_space=pltpu.SMEM)
    n_y = len(Y_FIRST)
    return pl.pallas_call(
        kernel,
        name="joint_attention",
        out_shape=(
            jax.ShapeDtypeStruct((32, WIDTH), F32),
            jax.ShapeDtypeStruct((32, WIDTH), F32),
        ),
        in_specs=[any_spec] * 6 + [smem_spec, vmem_spec, any_spec, any_spec],
        out_specs=(vmem_spec, vmem_spec),
        scratch_shapes=[
            vmem((4, 2, 256, LANES), BF),
            vmem((4, 2, 256, LANES), BF),
            vmem((4, 2, 256, LANES), BF),
            vmem((256, LANES), BF),
            vmem((256, LANES), BF),
            vmem((256, LANES), BF),
            vmem((256, LANES), BF),
            vmem((LANES, WIDTH), BF),
            vmem((LANES, LANES), BF),
            vmem((HEADS_HERE, 256, 2 * HD), F32),
            vmem((HEADS_HERE, 256, HD), F32),
            vmem((256, LANES), BF),
            vmem((2, 4, 32, WIDTH), BF),
            dma((11, 2, CHUNKS)),
            dma((12, 2, CHUNKS)),
            dma((8,)),
            vmem((2, 8, 16, 512), BF),
            vmem((8, 16, 512), BF),
            vmem((2, 4, 16, 512), BF),
            vmem((4, 16, 512), BF),
            vmem((2, 2, 16, 512), BF),
            vmem((2, 16, 512), BF),
            vmem((4, 8, 512), F32),
            vmem((4, 8, 512), F32),
            vmem((8, 8, LANES), F32),
            vmem((8, 8, LANES), F32),
            vmem((7, 8, LANES), F32),
            vmem((2, 2, 4, 2, 8, LANES), F32),
            dma((6,)),
            dma((4,)),
            dma((4,)),
            dma((7,)),
            dma((7,)),
            dma((7,)),
            dma((7,)),
            dma((7,)),
            dma((7,)),
            vmem((1, 4, 32, 1024), BF),
            vmem((1, 1, 4, 32, 1024), BF),
            vmem((n_y + 1, 2, 2, 32, 512), BF),
            vmem((n_y + 1, 2, 2, 2, 32, 512), BF),
            vmem((n_y + 1, 2, 2, 32, 512), BF),
            vmem((n_y, 2, 32, 1024), BF),
            vmem((n_y, 32, 1024), BF),
            dma((2, 1)),
            dma((n_y + 1, 6)),
            dma((n_y + 1, 6)),
            dma((2, n_y)),
        ],
        compiler_params=pltpu.CompilerParams(
            collective_id=0, has_side_effects=True, vmem_limit_bytes=56 * 2**20
        ),
        cost_estimate=pl.CostEstimate(flops=2_000_000_000, bytes_accessed=8_000_000, transcendentals=2_500_000),
    )(
        video_q, video_k, video_v, text_q, text_k, text_v, band_start, text_mask.reshape(1, TXT),
        video_proj, text_proj,
    )


def solution(mesh):
    return jax.shard_map(
        body,
        mesh=mesh,
        in_specs=(
            P("frm", "head"), P("frm", "head"), P("frm", "head"),
            P(None, "head"), P(None, "head"), P(None, "head"),
            P("frm"), P(), P("head", None), P("head", None),
        ),
        out_specs=(P(("frm", "head"), None), P("head", None)),
        check_vma=False,
    )
```

time: 498 us -> 77.9 us (0.16); the launches traced: 492 us -> 77.7 us
  blocking collectives: 112 us -> 0 us
  waiting for transfers between devices: 106 us -> 0 us
  starting transfers between devices: 88.9 us -> 0 us
  local copies, waits for them, and re-layouts: 85.2 us -> 3.53 us
  Pallas kernels: 0 us -> 72.9 us
  other arithmetic: 51.6 us -> 0 us
  matrix products: 28.8 us -> 0 us
  between operations: 18.7 us -> 1.29 us
    all_gather x2 -> x0, blocking collectives: 112 us -> none  [combined_all(): pieces = jax.tree.map(lambda part: lax.all_gather(part, axis), value)]
    ppermute x24 -> x0, starting transfers between devices: 88.8 us -> none  [shifted(): return lax.ppermute(array, axis, pairs)]
    pallas_call x0 -> x1, Pallas kernels: none -> 72.9 us  [body(): pl.pallas_call(kernel, name='joint_attention', out_shape=(jax.ShapeDtypeS...]
    reduce_scatter x2 -> x0, waiting for transfers between devices: 60.9 us -> none  [the longest x1 60.9 us: body(): lax.psum_scatter(jnp.dot(picked, text_proj, preferred_element_type=jnp.fl...]
    ppermute x24 -> x0, waiting for transfers between devices: 44.9 us -> none  [shifted(): return lax.ppermute(array, axis, pairs)]
    add x32 -> x0, other arithmetic: 39.2 us -> none  [the longest x31 39.1 us: merge_parts(): mixed_one * jnp.transpose(factor_one)[:, :, None]]
    dynamic_slice x31 -> x0, local copies, waits for them, and re-layouts: 32.1 us -> none  [combined_all(): lax.scan(lambda subtotal, piece: (join(subtotal, piece), None), head, tail)]
    dot_general x34 -> x0, matrix products: 28.8 us -> none  [the longest x16 15.5 us: partial_block(): jnp.einsum('qhd,khd->hqk', queries, key_block, preferred_element_type=jnp...]
  transfers between devices with their start and end apart: 27 -> 0, of which waited for: 7 -> 0; matrix products, arithmetic and copies ran while one was open for 32% -> 0% of each run, Pallas kernels for 0% -> 0%
where the time goes in v1:
time: 77.9 us; the launch traced here: 77.7 us
  Pallas kernels  72.9 us (94%)
  local copies, waits for them, and re-layouts  3.53 us (5%)
  between operations  1.29 us (2%)
    pallas_call x1, Pallas kernels, body(): pl.pallas_call(kernel, name='joint_attention', out_shape=(jax.ShapeDtypeS...  72.9 us
    unnamed x2, local copies, waits for them, and re-layouts  3.53 us

profile of v1, /device:TPU:1, one launch (start us, length us, event | category | flops | bytes accessed | tf_op | source)
XLA Modules:
  0.0 77.7 jit_solution(2543831665724602811)
XLA Ops:
  1.3 72.9 %joint_attention.1 = (f32[32,3072]{1,0:T(8,128)}, f32[32,3072]{1,0:T(8,128)}) custom-call(bf16[256,384]{1,0:T(8,128)(2,1)} %vq_hbm.1, bf16[256,384]{1,0:T(8,128)(2,1)} %vk_hbm.1, bf16[256,384]{1,0:T(8,128)(2,1)} %vv_hbm.1, bf16[256,384]{1,0:T(8,128)(2,1)} %tq_hbm.1, bf16[256,384]{1,0:T(8,128)(2,1)} %tk_hbm.1, bf16[256,384]{1,0:T(8,128)(2,1)} %tv_hbm.1, ...), custom_call_target="tpu_custom_call" | custom-call | flops 2000000000 | bytes 8000000 | tf_op jit(solution)/shard_map/joint_attention/pallas_call | solution.py:605
  74.2 1.8 %copy.15 = f32[32,3072]{1,0:T(8,128)} copy(f32[32,3072]{1,0:T(8,128)} %get-tuple-element.4) | data formatting | bytes 786432
  75.9 1.8 %copy.16 = f32[32,3072]{1,0:T(8,128)} copy(f32[32,3072]{1,0:T(8,128)} %get-tuple-element.5) | data formatting | bytes 786432

commit v2 on v0

v2 whole, which is shorter than its diff:
```python
import math

import jax
import jax.numpy as jnp
from jax import lax
from jax.experimental import pallas as pl
from jax.experimental.pallas import tpu as pltpu
from jax.sharding import PartitionSpec as P

HD = 128
TXT = 256
BANDS = 4
HEADS_HERE = 3
LANES = HEADS_HERE * HD
WIDTH = 3072
MESH = pl.DeviceIdType.MESH
BF = jnp.bfloat16
F32 = jnp.float32
FACTOR = math.log2(math.e) / math.sqrt(HD)
DEAD = -1e30
CHUNKS = 4
OWN, MATE, OPP, INTER, VMATE, VERT = range(6)
FAR = ((1, 2), (1, 3))
OPP_BY_MATE = ((1, 0), (1, 1), (1, 2))
PART = 768
HALF = PART // 2


def dot_nt(a, b):
    return lax.dot_general(a, b, (((1,), (1,)), ((), ())), preferred_element_type=F32)


def dot_nn(a, b):
    return jnp.dot(a, b, preferred_element_type=F32)


def with_ones(values):
    return jnp.concatenate([values, jnp.ones(values.shape, BF)], axis=1)


def kernel(
    vq_hbm, vk_hbm, vv_hbm, tq_hbm, tk_hbm, tv_hbm, band_hbm, mask_hbm, vproj_hbm, tproj_hbm,
    vout_ref, tout_ref,
    band_ref, mask_ref, k_a, k_b, k_c, v_a, v_b, v_c, vq, tq, tk, tv, vproj, tproj, state_o, state_m, weights_ref, attn, wpair, relay,
    kv_send, kv_recv, sib_recv, relay_recv, load_sem,
    t_a, t_ar, t_b, t_br, t_c, t_cr, t_z, t_zr, t_rows, t_sums, t_sumr, t_out,
    ta_sem, tz_sem, tg_sem, ts_sem, to_sem,
    swap_in, keep, y_out, y_in, z_out, z_in,
    w_sem, swap_sem, y_send, y_recv, z_send, z_recv,
):
    frm = lax.axis_index("frm")
    head = lax.axis_index("head")
    zh, x, c = frm // 8, (frm // 2) % 4, frm % 2
    zl, y = head // 4, head % 4
    xr, xo = x // 2, x % 2

    def at(zh_, x_, c_):
        return {"frm": zh_ * 8 + x_ * 2 + c_, "head": head}

    def at_head(zl_, y_):
        return {"frm": frm, "head": zl_ * 4 + y_}

    x_mate = x + 1 - 2 * xo
    sib = at(zh, x, 1 - c)
    mate = at(zh, x_mate, c)
    inter = at(zh, 3 - x, c)
    z_pair = at_head(1 - zl, y)
    y_of = (y + 1 - 2 * (y % 2), 3 - y)
    y_opp = (y + 2) % 4
    y_pair = (at_head(zl, y_of[0]), at_head(zl, y_of[1]))
    zh_to = zh + 1 - 2 * xr
    v_send = (zh_to >= 0) & (zh_to <= 3)
    zh_from = zh - 1 + 2 * xr
    v_recv = (zh_from >= 0) & (zh_from <= 3)
    vert = at(jnp.clip(zh_to, 0, 3), x, c)
    far = at(jnp.clip(zh_from, 0, 3), x, c)

    def copy_to(src, dst, send, recv, device):
        return pltpu.make_async_remote_copy(
            src_ref=src, dst_ref=dst, send_sem=send, recv_sem=recv,
            device_id=device, device_id_type=MESH,
        )

    loads = []

    def load(src, dst):
        copy = pltpu.make_async_copy(src, dst, load_sem.at[len(loads)])
        copy.start()
        loads.append(copy)
        return copy

    load_own = [load(vk_hbm, k_a.at[0]), load(vv_hbm, v_a.at[0])]
    load_text = [
        load(tq_hbm, tq), load(tk_hbm, tk), load(tv_hbm, tv), load(mask_hbm, mask_ref), load(band_hbm, band_ref)
    ]
    load_q = load(vq_hbm, vq)
    load_vproj = load(vproj_hbm, vproj)
    load_tproj = load(tproj_hbm.at[:, pl.ds(pl.multiple_of(x * 768, 768), 768)], tproj)

    frm_partners = [sib]
    frm_partners += [at((zh + d) % 4, x, c) for d in range(1, 4)]
    frm_partners += [at(zh, (x + d) % 4, c) for d in range(1, 4)]
    head_partners = [
        ((zl + dz) % 2, (y + dy) % 4) for dz in range(2) for dy in range(4) if (dz, dy) != (0, 0)
    ]
    barrier = pltpu.get_barrier_semaphore()
    with jax.named_scope("barrier"):
        for device in frm_partners + [at_head(a, b) for a, b in head_partners]:
            pl.semaphore_signal(barrier, inc=1, device_id=device, device_id_type=MESH)
        pl.semaphore_wait(barrier, len(frm_partners) + len(head_partners))

    rows = 256 // CHUNKS
    sends = []

    def kv_copy(kind, t, j, src_slot, dst_slot, device, src=None):
        rng = pl.ds(j * rows, rows)
        return copy_to(
            kv_of[t][src_slot // 4].at[src_slot % 4, rng] if src is None else src.at[rng],
            kv_of[t][dst_slot // 4].at[dst_slot % 4, rng],
            kv_send.at[kind],
            sib_recv.at[dst_slot // 2, t] if dst_slot % 2 else kv_recv.at[dst_slot // 2, t, j],
            device,
        )

    kv_of = ((k_a, k_b, k_c), (v_a, v_b, v_c))
    pieces = [(t, j) for t in range(2) for j in range(CHUNKS)]
    own_hbm = (vk_hbm, vv_hbm)

    def to_mate(t, j):
        return kv_copy(0, t, j, 0, 2 * MATE, mate, own_hbm[t])

    def to_inter(t, j):
        return kv_copy(1, t, j, 0, 2 * INTER, inter, own_hbm[t])

    def to_opp(t, j):
        if (t, j) in OPP_BY_MATE:
            return kv_copy(2, t, j, 2 * INTER, 2 * OPP, mate)
        return kv_copy(2, t, j, 2 * MATE, 2 * OPP, inter)

    def to_far(which, t, j):
        k = FAR.index((t, j))
        rng = pl.ds(j * rows, rows)
        return copy_to(
            own_hbm[t].at[rng] if which == 0 else kv_of[t][0].at[2 * MATE, rng],
            relay.at[which, k], kv_send.at[11 + which], relay_recv.at[which, k], far,
        )

    def to_relayed(which, t, j):
        k = FAR.index((t, j))
        role = (VERT, VMATE)[which]
        return copy_to(
            relay.at[which, k], kv_of[t][2].at[2 * role % 4, pl.ds(j * rows, rows)],
            kv_send.at[13 + which], kv_recv.at[role, t, j], inter,
        )

    def to_vert(t, j):
        return kv_copy(3, t, j, 2 * INTER, 2 * VERT, vert)

    def to_vmate(t, j):
        return kv_copy(4, t, j, 2 * VERT, 2 * VMATE, mate)

    def to_sib(role, t, j):
        return kv_copy(5 + role, t, j, 2 * role, 2 * role + 1, sib, own_hbm[t] if role == OWN else None)

    def go(copy):
        copy.start()
        sends.append(copy)

    def wait_bytes(ref, sem):
        copy_to(ref, ref, sem, kv_recv.at[0, 0, 0], sib).wait_send()

    def send_own(todo):
        for t, j in todo:
            to_inter(t, j).start()
            to_mate(t, j).start()
            to_sib(OWN, t, j).start()

    send_own(pieces[:CHUNKS])

    @pl.when(v_recv)
    def _():
        for t, j in FAR:
            to_far(0, t, j).start()

    def to_pair(pair):
        cols = pl.ds(pl.multiple_of(2 * PART * pair + PART * c, PART), PART)
        return copy_to(vproj_hbm.at[:, cols], wpair.at[pair, c], w_sem.at[0], w_sem.at[1 + pair], y_pair[pair])

    def pair_to_sib(pair):
        return copy_to(wpair.at[pair, c], wpair.at[pair, c], w_sem.at[3], w_sem.at[4], sib)

    for pair in range(2):
        to_pair(pair).start()

    for copy in load_own + load_text:
        copy.wait()
    lane = lax.broadcasted_iota(jnp.int32, (1, TXT), 1)
    text_bias = jnp.where(mask_ref[...] == 1, 0.0, DEAD)
    first_bias = jnp.where(frm == 0, text_bias, DEAD)

    def pack_stats(tops, totals):
        count = tops[0].shape[0]
        at_lane = lax.broadcasted_iota(jnp.int32, (count, HD), 1)
        packed = jnp.zeros((count, HD), F32)
        for h in range(HEADS_HERE):
            high = totals[h].astype(BF).astype(F32)
            packed = jnp.where(at_lane == h, tops[h], packed)
            packed = jnp.where(at_lane == 3 + h, high, packed)
            packed = jnp.where(at_lane == 6 + h, totals[h] - high, packed)
        return packed

    def text_partial():
        tops, totals, mixed = [], [], []
        for h in range(HEADS_HERE):
            cols = slice(h * HD, (h + 1) * HD)
            s_own = dot_nt(tq[:, cols], k_a[0, :, cols])
            s_text = dot_nt(tq[:, cols], tk[:, cols]) + first_bias
            top = jnp.maximum(
                jnp.max(s_own, axis=1, keepdims=True), jnp.max(s_text, axis=1, keepdims=True)
            ).astype(BF).astype(F32)
            base = top * FACTOR
            w_own = jnp.exp2(s_own * FACTOR - base).astype(BF)
            w_text = jnp.exp2(s_text * FACTOR - base).astype(BF)
            both = dot_nn(w_own, with_ones(v_a[0, :, cols])) + dot_nn(w_text, with_ones(tv[:, cols]))
            tops.append(top)
            totals.append(both[:, HD:HD + 1])
            mixed.append(both[:, :HD].astype(BF))
        stats = pack_stats(tops, totals).astype(BF)
        for h_to in range(8):
            for half in range(2):
                rng = slice(32 * h_to + 16 * half, 32 * h_to + 16 * half + 16)
                for h in range(HEADS_HERE):
                    t_a[half, h_to, :, h * HD:(h + 1) * HD] = mixed[h][rng]
                t_a[half, h_to, :, LANES:] = stats[rng]

    with jax.named_scope("text_partial"):
        text_partial()
    text_a = copy_to(t_a.at[1 - c], t_ar, ta_sem.at[0], ta_sem.at[1], sib)
    go(text_a)

    def merge(parts):
        parts = [p.astype(F32) for p in parts]
        out_tops, out_totals, out_mixed = [], [], []
        for h in range(HEADS_HERE):
            tops_h = [p[:, LANES + h:LANES + h + 1] for p in parts]
            top = tops_h[0]
            for other in tops_h[1:]:
                top = jnp.maximum(top, other)
            total, mix = 0.0, 0.0
            for p, top_p in zip(parts, tops_h):
                weight = jnp.exp2((top_p - top) * FACTOR)
                total_p = p[:, LANES + 3 + h:LANES + 4 + h] + p[:, LANES + 6 + h:LANES + 7 + h]
                total = total + total_p * weight
                mix = mix + p[:, h * HD:(h + 1) * HD] * weight
            out_tops.append(top)
            out_totals.append(total)
            out_mixed.append(mix)
        return out_tops, out_totals, out_mixed

    def merged(parts):
        out_tops, out_totals, out_mixed = merge(parts)
        return jnp.concatenate(out_mixed + [pack_stats(out_tops, out_totals)], axis=1)

    def slots_of_window():
        mid = c != xo
        pick_same = mid & (band_ref[0] == xo)
        return (0, jnp.where(mid, 3, 1), jnp.where(pick_same, 1, 2))

    def group_scores(g, with_text):
        slots = slots_of_window()
        for h in range(HEADS_HERE):
            cols = slice(h * HD, (h + 1) * HD)
            query = vq[:, cols]
            scores = [dot_nt(query, kv_of[0][g][s, :, cols]) for s in slots]
            if with_text:
                scores.append(dot_nt(query, tk[:, cols]) + text_bias)
            top = scores[0]
            for score in scores[1:]:
                top = jnp.maximum(top, score)
            top = jnp.max(top, axis=1, keepdims=True)
            base = top * FACTOR
            for i, score in enumerate(scores):
                weights_ref[g, h, i] = jnp.exp2(score * FACTOR - base).astype(BF)
            state_m[g, h] = jnp.broadcast_to(top, (256, HD))

    def group_values(g, with_text):
        slots = slots_of_window()
        for h in range(HEADS_HERE):
            cols = slice(h * HD, (h + 1) * HD)
            total = dot_nn(weights_ref[g, h, 0], with_ones(kv_of[1][g][slots[0], :, cols]))
            for i in (1, 2):
                total = total + dot_nn(weights_ref[g, h, i], with_ones(kv_of[1][g][slots[i], :, cols]))
            if with_text:
                total = total + dot_nn(weights_ref[g, h, 3], with_ones(tv[:, cols]))
            state_o[g, h] = total

    def join_groups():
        for h in range(HEADS_HERE):
            tops = [state_m[g, h] for g in range(3)]
            top = jnp.maximum(jnp.maximum(tops[0], tops[1]), tops[2])
            mix, total = 0.0, 0.0
            for g in range(3):
                factor = jnp.exp2((tops[g] - top) * FACTOR)
                mix = mix + state_o[g, h, :, :HD] * factor
                total = total + state_o[g, h, :, HD:] * factor
            attn[:, :, :, h * HD:(h + 1) * HD] = (mix / total).astype(BF).reshape(2, 4, 32, HD)

    def serve_inter(t, j):
        to_inter(t, j).wait_recv()
        to_sib(INTER, t, j).start()
        if (t, j) in OPP_BY_MATE:
            to_opp(t, j).start()

    def serve_mate(t, j):
        to_mate(t, j).wait_recv()
        if (t, j) in FAR:
            @pl.when(v_recv)
            def _():
                to_far(1, t, j).start()

        to_sib(MATE, t, j).start()
        if (t, j) not in OPP_BY_MATE:
            to_opp(t, j).start()

    def pass_own(t, j):
        @pl.when(v_send)
        def _():
            to_far(0, t, j).wait_recv()
            to_relayed(0, t, j).start()

    def pass_mate(t, j):
        @pl.when(v_send)
        def _():
            to_far(1, t, j).wait_recv()
            to_relayed(1, t, j).start()

    def serve_far(t, j):
        @pl.when(v_recv)
        def _():
            to_relayed(0, t, j).wait_recv()
            to_sib(VERT, t, j).start()
            to_relayed(1, t, j).wait_recv()
            to_sib(VMATE, t, j).start()

    def send_vert(t, j):
        @pl.when(v_send)
        def _():
            to_vert(t, j).start()

    def text_step_a():
        text_a.wait_recv()
        for h_to in range(8):
            t_b[h_to // 4, h_to % 4] = merged([t_a[c, h_to], t_ar[h_to]]).astype(BF)
        copy = copy_to(t_b.at[1 - xr], t_br, ta_sem.at[2], ta_sem.at[3], inter)
        go(copy)
        return copy

    def text_step_b(copy):
        copy.wait_recv()
        for k in range(4):
            t_c[k // 2, k % 2] = merged([t_b[xr, k], t_br[k]]).astype(BF)
        copy = copy_to(t_c.at[1 - xo], t_cr, ta_sem.at[4], ta_sem.at[5], mate)
        go(copy)
        return copy

    def text_step_c(copy):
        copy.wait_recv()
        for k in range(2):
            t_z[k] = merged([t_c[xo, k], t_cr[k]]).astype(BF)
        for dz in range(1, 4):
            copy_to(t_z, t_zr.at[dz], tz_sem.at[0], tz_sem.at[1], at((zh + dz) % 4, x, c)).start()

    def text_step_z():
        block = t_zr.at[pl.ds(1, 3)]
        copy_to(block, block, tz_sem.at[0], tz_sem.at[1], sib).wait_recv()
        for k in range(2):
            _, sums, mix = merge([t_z[k], t_zr[1, k], t_zr[2, k], t_zr[3, k]])
            for h in range(HEADS_HERE):
                t_rows[x, k, :, h * HD:(h + 1) * HD] = (mix[h] / sums[h]).astype(BF)
        for dx in range(1, 4):
            copy_to(t_rows.at[x], t_rows.at[x], tg_sem.at[0], tg_sem.at[1], at(zh, (x + dx) % 4, c)).start()

    def text_gather():
        block = t_rows.at[pl.ds(0, 3)]
        copy_to(block, block, tg_sem.at[0], tg_sem.at[1], sib).wait_recv()
        load_tproj.wait()
        rows_all = t_rows[...].reshape(128, LANES)
        product = dot_nn(rows_all, tproj[...]).astype(BF)
        for k in range(8):
            t_sums[k] = product[16 * k:16 * k + 16]
        for k, (a, b) in enumerate(head_partners):
            copy_to(t_sums.at[a * 4 + b], t_sumr.at[k], ts_sem.at[0], ts_sem.at[1], at_head(a, b)).start()

    def text_sum():
        copy_to(t_sumr, t_sumr, ts_sem.at[0], ts_sem.at[1], sib).wait_recv()
        total = t_sums[head].astype(F32)
        for k in range(7):
            total = total + t_sumr[k].astype(F32)
        t_out[c, x] = total
        for dx in range(1, 4):
            block = t_out.at[c, x]
            copy_to(block, block, to_sem.at[0], to_sem.at[1], at(zh, (x + dx) % 4, c)).start()

    def text_spread_sib():
        block = t_out.at[c, pl.ds(0, 3)]
        copy_to(block, block, to_sem.at[0], to_sem.at[1], sib).wait_recv()
        go(copy_to(t_out.at[c], t_out.at[c], to_sem.at[2], to_sem.at[3], sib))

    def text_finish():
        block = t_out.at[1 - c]
        copy_to(block, block, to_sem.at[2], to_sem.at[3], sib).wait_recv()
        for cc in range(2):
            for k in range(4):
                tout_ref[16 * cc:16 * cc + 16, k * 768:(k + 1) * 768] = t_out[cc, k]

    def serve_vert(t, j):
        @pl.when(v_recv)
        def _():
            to_vert(t, j).wait_recv()
            to_vmate(t, j).start()
            to_sib(VERT, t, j).start()

    def serve_vmate(t, j):
        @pl.when(v_recv)
        def _():
            to_vmate(t, j).wait_recv()
            to_sib(VMATE, t, j).start()

    def wait_sib(roles, t):
        for role in roles:
            block = kv_of[t][(2 * role + 1) // 4].at[(2 * role + 1) % 4]
            copy_to(block, block, kv_send.at[0], sib_recv.at[role, t], sib).wait_recv()

    def wait_sib_vert(t):
        @pl.when(v_recv)
        def _():
            wait_sib((VERT, VMATE), t)

    def serve_opp(t, j):
        to_opp(t, j).wait_recv()
        to_sib(OPP, t, j).start()

    scope = jax.named_scope
    def many(step, todo):
        with scope(step.__name__):
            for p in todo:
                step(*p)

    def part_of(todo, lo, hi):
        return todo[lo * CHUNKS // 4:hi * CHUNKS // 4]

    def first_hop(p, near):
        many(serve_inter, [p])
        if near:
            many(send_vert, [p])
        many(serve_mate, [p])

    k0, k1, k2, k3, v0, v1, v2, v3 = pieces
    first_hop(k0, True)
    with scope("text_sibling_merge"):
        text_copy = text_step_a()
        send_own(pieces[CHUNKS:])
    for p in (k1, k2, k3):
        first_hop(p, True)
    with scope("text_inter_merge"):
        text_copy = text_step_b(text_copy)
    first_hop(v0, True)
    first_hop(v1, True)
    many(pass_own, FAR)
    first_hop(v2, False)
    first_hop(v3, False)
    many(serve_vert, [k0, k1])
    with scope("text_mate_merge"):
        text_step_c(text_copy)
    with scope("wait_own_frame"):
        load_q.wait()
        wait_sib((OWN, MATE), 0)
        wait_sib((OWN, MATE), 1)
    with scope("own_frame"):
        group_scores(0, True)
        group_values(0, True)
    many(serve_vert, [k2, k3])
    many(serve_vmate, [k0])
    many(serve_opp, [k0, k1])
    many(pass_mate, FAR)
    with scope("projection_halves"):
        for pair in range(2):
            to_pair(pair).wait_recv()
            pair_to_sib(pair).start()
    many(serve_vert, [v0])
    many(serve_opp, [k2, k3])
    many(serve_vmate, [k1, k2])
    with scope("wait_beside_keys"):
        wait_sib((OPP, INTER), 0)
    with scope("frame_beside_scores"):
        group_scores(1, False)
    many(serve_vmate, [k3])
    many(serve_vert, [v1])
    with scope("wait_across_keys"):
        wait_sib_vert(0)
    with scope("frame_across_scores"):
        @pl.when(v_recv)
        def _():
            group_scores(2, False)

        @pl.when(jnp.logical_not(v_recv))
        def _():
            state_m[2] = jnp.full((HEADS_HERE, 256, HD), DEAD, F32)
            state_o[2] = jnp.zeros((HEADS_HERE, 256, 2 * HD), F32)
    many(serve_opp, [v0, v1, v2, v3])
    many(serve_vmate, [v0])
    with scope("text_z_merge"):
        text_step_z()
    many(serve_far, FAR)
    many(serve_vmate, [v1])
    with scope("wait_beside_values"):
        wait_sib((OPP, INTER), 1)
    with scope("frame_beside_values"):
        group_values(1, False)
    with scope("wait_across_values"):
        wait_sib_vert(1)
    with scope("frame_across_values"):
        @pl.when(v_recv)
        def _():
            group_values(2, False)
    with scope("join_groups"):
        join_groups()
    swap_own, swap_pair = [attn.at[:, y_of[0]], attn.at[:, y_of[1]]], attn.at[:, y_opp]
    for pair in range(2):
        copy_to(swap_own[pair], swap_in.at[pair, 0], swap_sem.at[0], swap_sem.at[1 + pair], y_pair[pair]).start()
        copy_to(swap_pair, swap_in.at[pair, 1], swap_sem.at[0], swap_sem.at[1 + pair], y_pair[pair]).start()

    with scope("text_gather"):
        text_gather()

    def own_rows(pair):
        return jnp.concatenate(
            [attn[:, y].reshape(64, LANES), attn[:, y_of[1 - pair]].reshape(64, LANES)], axis=0
        )

    with scope("project_own"):
        load_vproj.wait()
        for pair in range(2):
            rows_here = own_rows(pair)
            for q in range(2):
                lo = (2 * pair + q) * PART
                product = dot_nn(rows_here, vproj[:, lo:lo + PART])
                keep[pair, 2 * q], keep[pair, 2 * q + 1] = product[:, :HALF], product[:, HALF:]
        copy_to(wpair.at[0], wpair.at[0], w_sem.at[3], w_sem.at[4], sib).wait_recv()
    parts_of = [(pair, q) for q in range(4) for pair in range(2)]
    for pair in range(2):
        with scope("swap_wait"):
            copy_to(swap_in.at[pair], swap_in.at[pair], swap_sem.at[0], swap_sem.at[1 + pair], sib).wait_recv()
    for pair, q in parts_of:
        if q % 2 == 0:
            with scope("project_pair"):
                product = dot_nn(swap_in[pair].reshape(128, LANES), wpair[pair, q // 2])
                for k in range(2):
                    total = keep[pair, q + k] + product[:, k * HALF:(k + 1) * HALF]
                    y_out[pair, q + k] = total[64:].astype(BF)
                    keep[pair, q + k, :64] = total[:64]
                    copy_to(
                        y_out.at[pair, q + k], y_in.at[pair, q + k], y_send.at[0], y_recv.at[pair, q + k],
                        y_pair[1 - pair],
                    ).start()
    for pair, q in parts_of:
        if (pair, q) == parts_of[4]:
            with scope("text_sum"):
                text_sum()
        with scope("y_wait"):
            came = y_in.at[pair, q]
            copy_to(came, came, y_send.at[0], y_recv.at[pair, q], sib).wait_recv()
        with scope("y_sum"):
            lo = (4 * pair + q) * HALF
            total = keep[pair, q, :64] + y_in[pair, q].astype(F32)
            vout_ref[:, lo:lo + HALF] = jnp.where(zl == 0, total[:32], total[32:])
            z_out[pair, q] = jnp.where(zl == 0, total[32:], total[:32]).astype(BF)
        copy_to(z_out.at[pair, q], z_in.at[pair, q], z_send.at[0], z_recv.at[pair, q], z_pair).start()
    for pair, q in parts_of:
        if (pair, q) == parts_of[4]:
            with scope("text_spread_sib"):
                text_spread_sib()
        with scope("z_wait"):
            came = z_in.at[pair, q]
            copy_to(came, came, z_send.at[0], z_recv.at[pair, q], sib).wait_recv()
        lo = (4 * pair + q) * HALF
        vout_ref[:, lo:lo + HALF] = vout_ref[:, lo:lo + HALF] + z_in[pair, q].astype(F32)
    with scope("text_finish"):
        text_finish()

    with scope("wait_sends"):
        for copy in sends:
            copy.wait_send()

        whole = k_a.at[pl.ds(0, 2)]
        for kind in (0, 1, 2, 5 + OWN, 5 + MATE, 5 + OPP, 5 + INTER):
            wait_bytes(whole, kv_send.at[kind])

        most, quarter = k_a.at[pl.ds(0, 3), pl.ds(0, 128)], k_a.at[0, pl.ds(0, 128)]

        @pl.when(v_send)
        def _():
            wait_bytes(most, kv_send.at[3])
            wait_bytes(quarter, kv_send.at[13])
            wait_bytes(quarter, kv_send.at[14])

        @pl.when(v_recv)
        def _():
            wait_bytes(most, kv_send.at[4])
            wait_bytes(whole, kv_send.at[5 + VERT])
            wait_bytes(whole, kv_send.at[5 + VMATE])
            wait_bytes(quarter, kv_send.at[11])
            wait_bytes(quarter, kv_send.at[12])

        wait_bytes(t_zr.at[pl.ds(1, 3)], tz_sem.at[0])
        wait_bytes(t_rows.at[pl.ds(0, 3)], tg_sem.at[0])
        wait_bytes(t_sumr, ts_sem.at[0])
        wait_bytes(t_out.at[0, pl.ds(0, 3)], to_sem.at[0])
        wait_bytes(wpair.at[0], w_sem.at[0])
        wait_bytes(wpair.at[0], w_sem.at[3])
        wait_bytes(swap_in, swap_sem.at[0])
        wait_bytes(y_in, y_send.at[0])
        wait_bytes(z_in, z_send.at[0])


def store(video, text, video_out, text_out, sems):
    copies = [
        pltpu.make_async_copy(video, video_out, sems.at[0]),
        pltpu.make_async_copy(text, text_out, sems.at[1]),
    ]
    for copy in copies:
        copy.start()
    for copy in copies:
        copy.wait()


def body(video_q, video_k, video_v, text_q, text_k, text_v, band_start, text_mask, video_proj, text_proj):
    dma = pltpu.SemaphoreType.DMA
    vmem = pltpu.VMEM
    hbm_spec = pl.BlockSpec(memory_space=pltpu.HBM)
    vmem_spec = pl.BlockSpec(memory_space=pltpu.VMEM)
    outs = pl.pallas_call(
        kernel,
        name="joint_attention",
        out_shape=(pltpu.VMEM((32, WIDTH), F32), pltpu.VMEM((32, WIDTH), F32)),
        in_specs=[hbm_spec] * 10,
        out_specs=(vmem_spec, vmem_spec),
        scratch_shapes=[
            pltpu.SMEM((1,), jnp.int32),
            vmem((1, TXT), jnp.int32),
            *[vmem((4, 256, LANES), BF) for _ in range(6)],
            vmem((256, LANES), BF),
            vmem((256, LANES), BF),
            vmem((256, LANES), BF),
            vmem((256, LANES), BF),
            vmem((LANES, WIDTH), BF),
            vmem((LANES, 768), BF),
            vmem((3, HEADS_HERE, 256, 2 * HD), F32),
            vmem((3, HEADS_HERE, 256, HD), F32),
            vmem((3, HEADS_HERE, 4, 256, 256), BF),
            vmem((2, 4, 32, LANES), BF),
            vmem((2, 2, LANES, PART), BF),
            vmem((2, len(FAR), 256 // CHUNKS, LANES), BF),
            dma((15,)),
            dma((6, 2, CHUNKS)),
            dma((6, 2)),
            dma((2, len(FAR))),
            dma((10,)),
            vmem((2, 8, 16, 512), BF),
            vmem((8, 16, 512), BF),
            vmem((2, 4, 16, 512), BF),
            vmem((4, 16, 512), BF),
            vmem((2, 2, 16, 512), BF),
            vmem((2, 16, 512), BF),
            vmem((2, 16, 512), BF),
            vmem((4, 2, 16, 512), BF),
            vmem((4, 2, 16, LANES), BF),
            vmem((8, 16, 768), BF),
            vmem((7, 16, 768), BF),
            vmem((2, 4, 16, 768), F32),
            dma((6,)),
            dma((2,)),
            dma((2,)),
            dma((2,)),
            dma((4,)),
            vmem((2, 2, 2, 32, LANES), BF),
            vmem((2, 4, 128, HALF), F32),
            vmem((2, 4, 64, HALF), BF),
            vmem((2, 4, 64, HALF), BF),
            vmem((2, 4, 32, HALF), BF),
            vmem((2, 4, 32, HALF), BF),
            dma((5,)),
            dma((3,)),
            dma((1,)),
            dma((2, 4)),
            dma((1,)),
            dma((2, 4)),
        ],
        compiler_params=pltpu.CompilerParams(
            collective_id=0, has_side_effects=True, vmem_limit_bytes=56 * 2**20
        ),
        cost_estimate=pl.CostEstimate(flops=2_000_000_000, bytes_accessed=8_000_000, transcendentals=2_500_000),
    )(
        video_q, video_k, video_v, text_q, text_k, text_v, band_start, text_mask.reshape(1, TXT),
        video_proj, text_proj,
    )
    result = jax.ShapeDtypeStruct((32, WIDTH), F32)
    return pl.pallas_call(
        store,
        name="store",
        out_shape=(result, result),
        in_specs=[vmem_spec, vmem_spec],
        out_specs=(hbm_spec, hbm_spec),
        scratch_shapes=[dma((2,))],
    )(*[pltpu.with_memory_space_constraint(out, pltpu.VMEM) for out in outs])


def solution(mesh):
    return jax.shard_map(
        body,
        mesh=mesh,
        in_specs=(
            P("frm", "head"), P("frm", "head"), P("frm", "head"),
            P(None, "head"), P(None, "head"), P(None, "head"),
            P("frm"), P(), P("head", None), P("head", None),
        ),
        out_specs=(P(("frm", "head"), None), P("head", None)),
        check_vma=False,
    )
```

time: 498 us -> 56.6 us (0.11); the launches traced: 492 us -> 56.5 us
  blocking collectives: 112 us -> 0 us
  waiting for transfers between devices: 106 us -> 0 us
  starting transfers between devices: 88.9 us -> 0 us
  local copies, waits for them, and re-layouts: 85.2 us -> 0 us
  Pallas kernels: 0 us -> 55.2 us
  other arithmetic: 51.6 us -> 0 us
  matrix products: 28.8 us -> 0 us
  between operations: 18.7 us -> 1.29 us
    all_gather x2 -> x0, blocking collectives: 112 us -> none  [combined_all(): pieces = jax.tree.map(lambda part: lax.all_gather(part, axis), value)]
    ppermute x24 -> x0, starting transfers between devices: 88.8 us -> none  [shifted(): return lax.ppermute(array, axis, pairs)]
    reduce_scatter x2 -> x0, waiting for transfers between devices: 60.9 us -> none  [the longest x1 60.9 us: body(): lax.psum_scatter(jnp.dot(picked, text_proj, preferred_element_type=jnp.fl...]
    pallas_call x0 -> x2, Pallas kernels: none -> 55.2 us  [the longest x1 54.3 us: body(): pl.pallas_call(kernel, name='joint_attention', out_shape=(pltpu.VMEM((32,...]
    ppermute x24 -> x0, waiting for transfers between devices: 44.9 us -> none  [shifted(): return lax.ppermute(array, axis, pairs)]
    add x32 -> x0, other arithmetic: 39.2 us -> none  [the longest x31 39.1 us: merge_parts(): mixed_one * jnp.transpose(factor_one)[:, :, None]]
    dynamic_slice x31 -> x0, local copies, waits for them, and re-layouts: 32.1 us -> none  [combined_all(): lax.scan(lambda subtotal, piece: (join(subtotal, piece), None), head, tail)]
    dot_general x34 -> x0, matrix products: 28.8 us -> none  [the longest x16 15.5 us: partial_block(): jnp.einsum('qhd,khd->hqk', queries, key_block, preferred_element_type=jnp...]
  transfers between devices with their start and end apart: 27 -> 0, of which waited for: 7 -> 0; matrix products, arithmetic and copies ran while one was open for 32% -> 0% of each run, Pallas kernels for 0% -> 0%
where the time goes in v2:
time: 56.6 us; the launch traced here: 56.5 us
  Pallas kernels  55.2 us (98%)
  between operations  1.29 us (2%)
    pallas_call x1, Pallas kernels, body(): pl.pallas_call(kernel, name='joint_attention', out_shape=(pltpu.VMEM((32,...  54.3 us

profile of v2, /device:TPU:1, one launch (start us, length us, event | category | flops | bytes accessed | tf_op | source)
XLA Modules:
  0.0 56.5 jit_solution(2152076465284073977)
XLA Ops:
  1.3 54.3 %joint_attention.1 = (f32[32,3072]{1,0:T(8,128)S(1)}, f32[32,3072]{1,0:T(8,128)S(1)}) custom-call(bf16[256,384]{1,0:T(8,128)(2,1)} %vq_hbm.1, bf16[256,384]{1,0:T(8,128)(2,1)} %vk_hbm.1, bf16[256,384]{1,0:T(8,128)(2,1)} %vv_hbm.1, bf16[256,384]{1,0:T(8,128)(2,1)} %tq_hbm.1, bf16[256,384]{1,0:T(8,128)(2,1)} %tk_hbm.1, bf16[256,384]{1,0:T(8,128)(2,1)} %tv_hbm.1, ...), custom_call_target="tpu_custom_call" | custom-call | flops 2000000000 | bytes 8000000 | tf_op jit(solution)/shard_map/joint_attention/pallas_call | solution.py:642
  55.6 0.9 %store.1 = (f32[32,3072]{1,0:T(8,128)}, f32[32,3072]{1,0:T(8,128)}) custom-call(f32[32,3072]{1,0:T(8,128)S(1)} %get-tuple-element.4.video, f32[32,3072]{1,0:T(8,128)S(1)} %get-tuple-element.5.text), custom_call_target="tpu_custom_call" | custom-call | tf_op jit(solution)/shard_map/store/pallas_call | solution.py:708

commit v3 on v2

--- a/solution.py
+++ b/solution.py
@@ -20,8 +20,15 @@
 DEAD = -1e30
 CHUNKS = 4
 OWN, MATE, OPP, INTER, VMATE, VERT = range(6)
-FAR = ((1, 2), (1, 3))
-OPP_BY_MATE = ((1, 0), (1, 1), (1, 2))
+PER = CHUNKS // 4
+
+
+def quarter(t, k):
+    return tuple((t, k * PER + i) for i in range(PER))
+
+
+FAR = quarter(1, 2) + quarter(1, 3)
+OPP_BY_MATE = quarter(1, 0) + quarter(1, 1) + quarter(1, 2)
 PART = 768
 HALF = PART // 2
 
@@ -169,13 +176,16 @@
     def wait_bytes(ref, sem):
         copy_to(ref, ref, sem, kv_recv.at[0, 0, 0], sib).wait_send()
 
-    def send_own(todo):
-        for t, j in todo:
-            to_inter(t, j).start()
-            to_mate(t, j).start()
-            to_sib(OWN, t, j).start()
-
-    send_own(pieces[:CHUNKS])
+    def send_own(todo_inter, todo_mate):
+        for p_inter, p_mate in zip(todo_inter, todo_mate):
+            to_inter(*p_inter).start()
+            to_mate(*p_mate).start()
+            to_sib(OWN, *p_mate).start()
+
+    (k0, k1, k2, k3), (v0, v1, v2, v3) = [[quarter(t, k) for k in range(4)] for t in range(2)]
+    order_inter = k0 + k1 + k2 + k3 + v0 + v1 + v2 + v3
+    order_mate = k0 + k1 + v2 + v3 + k2 + k3 + v0 + v1
+    send_own(order_inter[:CHUNKS], order_mate[:CHUNKS])
 
     @pl.when(v_recv)
     def _():
@@ -396,7 +406,7 @@
         total = t_sums[head].astype(F32)
         for k in range(7):
             total = total + t_sumr[k].astype(F32)
-        t_out[c, x] = total
+        t_out[c, x] = total.astype(BF)
         for dx in range(1, 4):
             block = t_out.at[c, x]
             copy_to(block, block, to_sem.at[0], to_sem.at[1], at(zh, (x + dx) % 4, c)).start()
@@ -411,7 +421,7 @@
         copy_to(block, block, to_sem.at[2], to_sem.at[3], sib).wait_recv()
         for cc in range(2):
             for k in range(4):
-                tout_ref[16 * cc:16 * cc + 16, k * 768:(k + 1) * 768] = t_out[cc, k]
+                tout_ref[16 * cc:16 * cc + 16, k * 768:(k + 1) * 768] = t_out[cc, k].astype(F32)
 
     def serve_vert(t, j):
         @pl.when(v_recv)
@@ -449,29 +459,30 @@
     def part_of(todo, lo, hi):
         return todo[lo * CHUNKS // 4:hi * CHUNKS // 4]
 
-    def first_hop(p, near):
-        many(serve_inter, [p])
-        if near:
-            many(send_vert, [p])
-        many(serve_mate, [p])
-
-    k0, k1, k2, k3, v0, v1, v2, v3 = pieces
-    first_hop(k0, True)
+    def first_hop(lo, hi):
+        for k in range(lo * PER, hi * PER):
+            many(serve_inter, [order_inter[k]])
+            if order_inter[k] not in FAR:
+                many(send_vert, [order_inter[k]])
+            many(serve_mate, [order_mate[k]])
+
+    first_hop(0, 1)
     with scope("text_sibling_merge"):
         text_copy = text_step_a()
-        send_own(pieces[CHUNKS:])
-    for p in (k1, k2, k3):
-        first_hop(p, True)
+        send_own(order_inter[CHUNKS:], order_mate[CHUNKS:])
+    first_hop(1, 4)
     with scope("text_inter_merge"):
         text_copy = text_step_b(text_copy)
-    first_hop(v0, True)
-    first_hop(v1, True)
+    first_hop(4, 6)
     many(pass_own, FAR)
-    first_hop(v2, False)
-    first_hop(v3, False)
-    many(serve_vert, [k0, k1])
     with scope("text_mate_merge"):
         text_step_c(text_copy)
+    first_hop(6, 8)
+    many(pass_mate, FAR)
+    many(serve_vert, k0 + k1)
+    many(serve_vert, k2)
+    many(serve_opp, k0 + k1)
+    many(serve_vert, k3)
     with scope("wait_own_frame"):
         load_q.wait()
         wait_sib((OWN, MATE), 0)
@@ -479,23 +490,23 @@
     with scope("own_frame"):
         group_scores(0, True)
         group_values(0, True)
-    many(serve_vert, [k2, k3])
-    many(serve_vmate, [k0])
-    many(serve_opp, [k0, k1])
-    many(pass_mate, FAR)
+    many(serve_vert, v0)
+    many(serve_opp, k2 + k3)
+    many(serve_vmate, k0 + k1 + k2)
     with scope("projection_halves"):
         for pair in range(2):
             to_pair(pair).wait_recv()
             pair_to_sib(pair).start()
-    many(serve_vert, [v0])
-    many(serve_opp, [k2, k3])
-    many(serve_vmate, [k1, k2])
+    many(serve_vert, v1)
     with scope("wait_beside_keys"):
         wait_sib((OPP, INTER), 0)
     with scope("frame_beside_scores"):
         group_scores(1, False)
-    many(serve_vmate, [k3])
-    many(serve_vert, [v1])
+    many(serve_vmate, k3)
+    many(serve_opp, v0 + v1 + v2 + v3)
+    with scope("text_z_merge"):
+        text_step_z()
+    many(serve_far, FAR)
     with scope("wait_across_keys"):
         wait_sib_vert(0)
     with scope("frame_across_scores"):
@@ -507,16 +518,12 @@
         def _():
             state_m[2] = jnp.full((HEADS_HERE, 256, HD), DEAD, F32)
             state_o[2] = jnp.zeros((HEADS_HERE, 256, 2 * HD), F32)
-    many(serve_opp, [v0, v1, v2, v3])
-    many(serve_vmate, [v0])
-    with scope("text_z_merge"):
-        text_step_z()
-    many(serve_far, FAR)
-    many(serve_vmate, [v1])
+    many(serve_vmate, v0)
     with scope("wait_beside_values"):
         wait_sib((OPP, INTER), 1)
     with scope("frame_beside_values"):
         group_values(1, False)
+    many(serve_vmate, v1)
     with scope("wait_across_values"):
         wait_sib_vert(1)
     with scope("frame_across_values"):
@@ -529,9 +536,6 @@
     for pair in range(2):
         copy_to(swap_own[pair], swap_in.at[pair, 0], swap_sem.at[0], swap_sem.at[1 + pair], y_pair[pair]).start()
         copy_to(swap_pair, swap_in.at[pair, 1], swap_sem.at[0], swap_sem.at[1 + pair], y_pair[pair]).start()
-
-    with scope("text_gather"):
-        text_gather()
 
     def own_rows(pair):
         return jnp.concatenate(
@@ -547,6 +551,8 @@
                 product = dot_nn(rows_here, vproj[:, lo:lo + PART])
                 keep[pair, 2 * q], keep[pair, 2 * q + 1] = product[:, :HALF], product[:, HALF:]
         copy_to(wpair.at[0], wpair.at[0], w_sem.at[3], w_sem.at[4], sib).wait_recv()
+    with scope("text_gather"):
+        text_gather()
     parts_of = [(pair, q) for q in range(4) for pair in range(2)]
     for pair in range(2):
         with scope("swap_wait"):
@@ -563,10 +569,9 @@
                         y_out.at[pair, q + k], y_in.at[pair, q + k], y_send.at[0], y_recv.at[pair, q + k],
                         y_pair[1 - pair],
                     ).start()
+    with scope("text_sum"):
+        text_sum()
     for pair, q in parts_of:
-        if (pair, q) == parts_of[4]:
-            with scope("text_sum"):
-                text_sum()
         with scope("y_wait"):
             came = y_in.at[pair, q]
             copy_to(came, came, y_send.at[0], y_recv.at[pair, q], sib).wait_recv()
@@ -576,18 +581,17 @@
             vout_ref[:, lo:lo + HALF] = jnp.where(zl == 0, total[:32], total[32:])
             z_out[pair, q] = jnp.where(zl == 0, total[32:], total[:32]).astype(BF)
         copy_to(z_out.at[pair, q], z_in.at[pair, q], z_send.at[0], z_recv.at[pair, q], z_pair).start()
+    with scope("text_spread_sib"):
+        text_spread_sib()
     for pair, q in parts_of:
-        if (pair, q) == parts_of[4]:
-            with scope("text_spread_sib"):
-                text_spread_sib()
         with scope("z_wait"):
             came = z_in.at[pair, q]
             copy_to(came, came, z_send.at[0], z_recv.at[pair, q], sib).wait_recv()
         lo = (4 * pair + q) * HALF
         vout_ref[:, lo:lo + HALF] = vout_ref[:, lo:lo + HALF] + z_in[pair, q].astype(F32)
+
     with scope("text_finish"):
         text_finish()
-
     with scope("wait_sends"):
         for copy in sends:
             copy.wait_send()
@@ -596,21 +600,21 @@
         for kind in (0, 1, 2, 5 + OWN, 5 + MATE, 5 + OPP, 5 + INTER):
             wait_bytes(whole, kv_send.at[kind])
 
-        most, quarter = k_a.at[pl.ds(0, 3), pl.ds(0, 128)], k_a.at[0, pl.ds(0, 128)]
+        most, fourth = k_a.at[pl.ds(0, 3), pl.ds(0, 128)], k_a.at[0, pl.ds(0, 128)]
 
         @pl.when(v_send)
         def _():
             wait_bytes(most, kv_send.at[3])
-            wait_bytes(quarter, kv_send.at[13])
-            wait_bytes(quarter, kv_send.at[14])
+            wait_bytes(fourth, kv_send.at[13])
+            wait_bytes(fourth, kv_send.at[14])
 
         @pl.when(v_recv)
         def _():
             wait_bytes(most, kv_send.at[4])
             wait_bytes(whole, kv_send.at[5 + VERT])
             wait_bytes(whole, kv_send.at[5 + VMATE])
-            wait_bytes(quarter, kv_send.at[11])
-            wait_bytes(quarter, kv_send.at[12])
+            wait_bytes(fourth, kv_send.at[11])
+            wait_bytes(fourth, kv_send.at[12])
 
         wait_bytes(t_zr.at[pl.ds(1, 3)], tz_sem.at[0])
         wait_bytes(t_rows.at[pl.ds(0, 3)], tg_sem.at[0])
@@ -677,7 +681,7 @@
             vmem((4, 2, 16, LANES), BF),
             vmem((8, 16, 768), BF),
             vmem((7, 16, 768), BF),
-            vmem((2, 4, 16, 768), F32),
+            vmem((2, 4, 16, 768), BF),
             dma((6,)),
             dma((2,)),
             dma((2,)),

time: 56.6 us -> 52.9 us (0.935); the launches traced: 56.5 us -> 52.2 us
  Pallas kernels: 55.2 us -> 50.9 us
    pallas_call x1, Pallas kernels: 54.3 us -> 50 us  [body(): pl.pallas_call(kernel, name='joint_attention', out_shape=(pltpu.VMEM((32,...]
where the time goes in v3:
time: 52.9 us; the launch traced here: 52.2 us
  Pallas kernels  50.9 us (96%)
  between operations  1.29 us (2%)
    pallas_call x1, Pallas kernels, body(): pl.pallas_call(kernel, name='joint_attention', out_shape=(pltpu.VMEM((32,...  50 us

profile of v3, /device:TPU:1, one launch (start us, length us, event | category | flops | bytes accessed | tf_op | source)
XLA Modules:
  0.0 52.2 jit_solution(14496246982743918767)
XLA Ops:
  1.3 50.0 %joint_attention.1 = (f32[32,3072]{1,0:T(8,128)S(1)}, f32[32,3072]{1,0:T(8,128)S(1)}) custom-call(bf16[256,384]{1,0:T(8,128)(2,1)} %vq_hbm.1, bf16[256,384]{1,0:T(8,128)(2,1)} %vk_hbm.1, bf16[256,384]{1,0:T(8,128)(2,1)} %vv_hbm.1, bf16[256,384]{1,0:T(8,128)(2,1)} %tq_hbm.1, bf16[256,384]{1,0:T(8,128)(2,1)} %tk_hbm.1, bf16[256,384]{1,0:T(8,128)(2,1)} %tv_hbm.1, ...), custom_call_target="tpu_custom_call" | custom-call | flops 2000000000 | bytes 8000000 | tf_op jit(solution)/shard_map/joint_attention/pallas_call | solution.py:646
  51.3 0.9 %store.1 = (f32[32,3072]{1,0:T(8,128)}, f32[32,3072]{1,0:T(8,128)}) custom-call(f32[32,3072]{1,0:T(8,128)S(1)} %get-tuple-element.4.video, f32[32,3072]{1,0:T(8,128)S(1)} %get-tuple-element.5.text), custom_call_target="tpu_custom_call" | custom-call | tf_op jit(solution)/shard_map/store/pallas_call | solution.py:712

commit v4 on v3

--- a/solution.py
+++ b/solution.py
@@ -50,7 +50,7 @@
     vout_ref, tout_ref,
     band_ref, mask_ref, k_a, k_b, k_c, v_a, v_b, v_c, vq, tq, tk, tv, vproj, tproj, state_o, state_m, weights_ref, attn, wpair, relay,
     kv_send, kv_recv, sib_recv, relay_recv, load_sem,
-    t_a, t_ar, t_b, t_br, t_c, t_cr, t_z, t_zr, t_rows, t_sums, t_sumr, t_out,
+    t_a, t_ar, t_b, t_br, t_c, t_cr, t_zr, t_rows, t_sums, t_sumr, t_out,
     ta_sem, tz_sem, tg_sem, ts_sem, to_sem,
     swap_in, keep, y_out, y_in, z_out, z_in,
     w_sem, swap_sem, y_send, y_recv, z_send, z_recv,
@@ -376,15 +376,15 @@
     def text_step_c(copy):
         copy.wait_recv()
         for k in range(2):
-            t_z[k] = merged([t_c[xo, k], t_cr[k]]).astype(BF)
+            t_zr[zh, k] = merged([t_c[xo, k], t_cr[k]]).astype(BF)
         for dz in range(1, 4):
-            copy_to(t_z, t_zr.at[dz], tz_sem.at[0], tz_sem.at[1], at((zh + dz) % 4, x, c)).start()
+            copy_to(t_zr.at[zh], t_zr.at[zh], tz_sem.at[0], tz_sem.at[1], at((zh + dz) % 4, x, c)).start()
 
     def text_step_z():
         block = t_zr.at[pl.ds(1, 3)]
         copy_to(block, block, tz_sem.at[0], tz_sem.at[1], sib).wait_recv()
         for k in range(2):
-            _, sums, mix = merge([t_z[k], t_zr[1, k], t_zr[2, k], t_zr[3, k]])
+            _, sums, mix = merge([t_zr[i, k] for i in range(4)])
             for h in range(HEADS_HERE):
                 t_rows[x, k, :, h * HD:(h + 1) * HD] = (mix[h] / sums[h]).astype(BF)
         for dx in range(1, 4):
@@ -466,11 +466,10 @@
                 many(send_vert, [order_inter[k]])
             many(serve_mate, [order_mate[k]])
 
-    first_hop(0, 1)
     with scope("text_sibling_merge"):
         text_copy = text_step_a()
         send_own(order_inter[CHUNKS:], order_mate[CHUNKS:])
-    first_hop(1, 4)
+    first_hop(0, 4)
     with scope("text_inter_merge"):
         text_copy = text_step_b(text_copy)
     first_hop(4, 6)
@@ -498,15 +497,18 @@
             to_pair(pair).wait_recv()
             pair_to_sib(pair).start()
     many(serve_vert, v1)
+    with scope("text_z_merge"):
+        text_step_z()
     with scope("wait_beside_keys"):
         wait_sib((OPP, INTER), 0)
     with scope("frame_beside_scores"):
         group_scores(1, False)
     many(serve_vmate, k3)
     many(serve_opp, v0 + v1 + v2 + v3)
-    with scope("text_z_merge"):
-        text_step_z()
     many(serve_far, FAR)
+    many(serve_vmate, v0 + v1)
+    with scope("text_gather"):
+        text_gather()
     with scope("wait_across_keys"):
         wait_sib_vert(0)
     with scope("frame_across_scores"):
@@ -518,12 +520,10 @@
         def _():
             state_m[2] = jnp.full((HEADS_HERE, 256, HD), DEAD, F32)
             state_o[2] = jnp.zeros((HEADS_HERE, 256, 2 * HD), F32)
-    many(serve_vmate, v0)
     with scope("wait_beside_values"):
         wait_sib((OPP, INTER), 1)
     with scope("frame_beside_values"):
         group_values(1, False)
-    many(serve_vmate, v1)
     with scope("wait_across_values"):
         wait_sib_vert(1)
     with scope("frame_across_values"):
@@ -551,8 +551,8 @@
                 product = dot_nn(rows_here, vproj[:, lo:lo + PART])
                 keep[pair, 2 * q], keep[pair, 2 * q + 1] = product[:, :HALF], product[:, HALF:]
         copy_to(wpair.at[0], wpair.at[0], w_sem.at[3], w_sem.at[4], sib).wait_recv()
-    with scope("text_gather"):
-        text_gather()
+    with scope("text_sum"):
+        text_sum()
     parts_of = [(pair, q) for q in range(4) for pair in range(2)]
     for pair in range(2):
         with scope("swap_wait"):
@@ -569,8 +569,8 @@
                         y_out.at[pair, q + k], y_in.at[pair, q + k], y_send.at[0], y_recv.at[pair, q + k],
                         y_pair[1 - pair],
                     ).start()
-    with scope("text_sum"):
-        text_sum()
+    with scope("text_spread_sib"):
+        text_spread_sib()
     for pair, q in parts_of:
         with scope("y_wait"):
             came = y_in.at[pair, q]
@@ -581,8 +581,6 @@
             vout_ref[:, lo:lo + HALF] = jnp.where(zl == 0, total[:32], total[32:])
             z_out[pair, q] = jnp.where(zl == 0, total[32:], total[:32]).astype(BF)
         copy_to(z_out.at[pair, q], z_in.at[pair, q], z_send.at[0], z_recv.at[pair, q], z_pair).start()
-    with scope("text_spread_sib"):
-        text_spread_sib()
     for pair, q in parts_of:
         with scope("z_wait"):
             came = z_in.at[pair, q]
@@ -675,7 +673,6 @@
             vmem((2, 4, 16, 512), BF),
             vmem((4, 16, 512), BF),
             vmem((2, 2, 16, 512), BF),
-            vmem((2, 16, 512), BF),
             vmem((2, 16, 512), BF),
             vmem((4, 2, 16, 512), BF),
             vmem((4, 2, 16, LANES), BF),

time: 52.9 us -> 52.2 us (0.987)
  the two profiles are of different devices: /device:TPU:1 before, /device:TPU:32 now
where the time goes in v4:
time: 52.2 us; the launch traced here: 52.1 us
  Pallas kernels  50.8 us (97%)
  between operations  1.29 us (2%)
    pallas_call x1, Pallas kernels, body(): pl.pallas_call(kernel, name='joint_attention', out_shape=(pltpu.VMEM((32,...  49.9 us

profile of v4, /device:TPU:32, one launch (start us, length us, event | category | flops | bytes accessed | tf_op | source)
XLA Modules:
  0.0 52.1 jit_solution(14702913953565961154)
XLA Ops:
  1.3 49.9 %joint_attention.1 = (f32[32,3072]{1,0:T(8,128)S(1)}, f32[32,3072]{1,0:T(8,128)S(1)}) custom-call(bf16[256,384]{1,0:T(8,128)(2,1)} %vq_hbm.1, bf16[256,384]{1,0:T(8,128)(2,1)} %vk_hbm.1, bf16[256,384]{1,0:T(8,128)(2,1)} %vv_hbm.1, bf16[256,384]{1,0:T(8,128)(2,1)} %tq_hbm.1, bf16[256,384]{1,0:T(8,128)(2,1)} %tk_hbm.1, bf16[256,384]{1,0:T(8,128)(2,1)} %tv_hbm.1, ...), custom_call_target="tpu_custom_call" | custom-call | flops 2000000000 | bytes 8000000 | tf_op jit(solution)/shard_map/joint_attention/pallas_call | solution.py:644
  51.2 0.9 %store.1 = (f32[32,3072]{1,0:T(8,128)}, f32[32,3072]{1,0:T(8,128)}) custom-call(f32[32,3072]{1,0:T(8,128)S(1)} %get-tuple-element.4.video, f32[32,3072]{1,0:T(8,128)S(1)} %get-tuple-element.5.text), custom_call_target="tpu_custom_call" | custom-call | tf_op jit(solution)/shard_map/store/pallas_call | solution.py:709

commit v5 on v4

--- a/solution.py
+++ b/solution.py
@@ -551,8 +551,6 @@
                 product = dot_nn(rows_here, vproj[:, lo:lo + PART])
                 keep[pair, 2 * q], keep[pair, 2 * q + 1] = product[:, :HALF], product[:, HALF:]
         copy_to(wpair.at[0], wpair.at[0], w_sem.at[3], w_sem.at[4], sib).wait_recv()
-    with scope("text_sum"):
-        text_sum()
     parts_of = [(pair, q) for q in range(4) for pair in range(2)]
     for pair in range(2):
         with scope("swap_wait"):
@@ -569,8 +567,8 @@
                         y_out.at[pair, q + k], y_in.at[pair, q + k], y_send.at[0], y_recv.at[pair, q + k],
                         y_pair[1 - pair],
                     ).start()
-    with scope("text_spread_sib"):
-        text_spread_sib()
+    with scope("text_sum"):
+        text_sum()
     for pair, q in parts_of:
         with scope("y_wait"):
             came = y_in.at[pair, q]
@@ -581,6 +579,8 @@
             vout_ref[:, lo:lo + HALF] = jnp.where(zl == 0, total[:32], total[32:])
             z_out[pair, q] = jnp.where(zl == 0, total[32:], total[:32]).astype(BF)
         copy_to(z_out.at[pair, q], z_in.at[pair, q], z_send.at[0], z_recv.at[pair, q], z_pair).start()
+    with scope("text_spread_sib"):
+        text_spread_sib()
     for pair, q in parts_of:
         with scope("z_wait"):
             came = z_in.at[pair, q]

time: 52.2 us -> 52.7 us (level)
  the two profiles are of different devices: /device:TPU:32 before, /device:TPU:1 now
where the time goes in v5:
time: 52.7 us; the launch traced here: 52.5 us
  Pallas kernels  51.2 us (97%)
  between operations  1.29 us (2%)
    pallas_call x1, Pallas kernels, body(): pl.pallas_call(kernel, name='joint_attention', out_shape=(pltpu.VMEM((32,...  50.3 us

profile of v5, /device:TPU:1, one launch (start us, length us, event | category | flops | bytes accessed | tf_op | source)
XLA Modules:
  0.0 52.5 jit_solution(2032911020568309610)
XLA Ops:
  1.3 50.3 %joint_attention.1 = (f32[32,3072]{1,0:T(8,128)S(1)}, f32[32,3072]{1,0:T(8,128)S(1)}) custom-call(bf16[256,384]{1,0:T(8,128)(2,1)} %vq_hbm.1, bf16[256,384]{1,0:T(8,128)(2,1)} %vk_hbm.1, bf16[256,384]{1,0:T(8,128)(2,1)} %vv_hbm.1, bf16[256,384]{1,0:T(8,128)(2,1)} %tq_hbm.1, bf16[256,384]{1,0:T(8,128)(2,1)} %tk_hbm.1, bf16[256,384]{1,0:T(8,128)(2,1)} %tv_hbm.1, ...), custom_call_target="tpu_custom_call" | custom-call | flops 2000000000 | bytes 8000000 | tf_op jit(solution)/shard_map/joint_attention/pallas_call | solution.py:644
  51.6 0.9 %store.1 = (f32[32,3072]{1,0:T(8,128)}, f32[32,3072]{1,0:T(8,128)}) custom-call(f32[32,3072]{1,0:T(8,128)S(1)} %get-tuple-element.4.video, f32[32,3072]{1,0:T(8,128)S(1)} %get-tuple-element.5.text), custom_call_target="tpu_custom_call" | custom-call | tf_op jit(solution)/shard_map/store/pallas_call | solution.py:709

commit v6 on v5

--- a/solution.py
+++ b/solution.py
@@ -551,6 +551,8 @@
                 product = dot_nn(rows_here, vproj[:, lo:lo + PART])
                 keep[pair, 2 * q], keep[pair, 2 * q + 1] = product[:, :HALF], product[:, HALF:]
         copy_to(wpair.at[0], wpair.at[0], w_sem.at[3], w_sem.at[4], sib).wait_recv()
+    with scope("text_sum"):
+        text_sum()
     parts_of = [(pair, q) for q in range(4) for pair in range(2)]
     for pair in range(2):
         with scope("swap_wait"):
@@ -567,8 +569,6 @@
                         y_out.at[pair, q + k], y_in.at[pair, q + k], y_send.at[0], y_recv.at[pair, q + k],
                         y_pair[1 - pair],
                     ).start()
-    with scope("text_sum"):
-        text_sum()
     for pair, q in parts_of:
         with scope("y_wait"):
             came = y_in.at[pair, q]

time: 52.7 us -> 52.6 us (level)
  no operation moved by 1% of the time
where the time goes in v6:
time: 52.6 us; the launch traced here: 52.5 us
  Pallas kernels  51.2 us (97%)
  between operations  1.29 us (2%)
    pallas_call x1, Pallas kernels, body(): pl.pallas_call(kernel, name='joint_attention', out_shape=(pltpu.VMEM((32,...  50.3 us

profile of v6, /device:TPU:1, one launch (start us, length us, event | category | flops | bytes accessed | tf_op | source)
XLA Modules:
  0.0 52.5 jit_solution(8603665462080540323)
XLA Ops:
  1.3 50.3 %joint_attention.1 = (f32[32,3072]{1,0:T(8,128)S(1)}, f32[32,3072]{1,0:T(8,128)S(1)}) custom-call(bf16[256,384]{1,0:T(8,128)(2,1)} %vq_hbm.1, bf16[256,384]{1,0:T(8,128)(2,1)} %vk_hbm.1, bf16[256,384]{1,0:T(8,128)(2,1)} %vv_hbm.1, bf16[256,384]{1,0:T(8,128)(2,1)} %tq_hbm.1, bf16[256,384]{1,0:T(8,128)(2,1)} %tk_hbm.1, bf16[256,384]{1,0:T(8,128)(2,1)} %tv_hbm.1, ...), custom_call_target="tpu_custom_call" | custom-call | flops 2000000000 | bytes 8000000 | tf_op jit(solution)/shard_map/joint_attention/pallas_call | solution.py:644
  51.6 0.9 %store.1 = (f32[32,3072]{1,0:T(8,128)}, f32[32,3072]{1,0:T(8,128)}) custom-call(f32[32,3072]{1,0:T(8,128)S(1)} %get-tuple-element.4.video, f32[32,3072]{1,0:T(8,128)S(1)} %get-tuple-element.5.text), custom_call_target="tpu_custom_call" | custom-call | tf_op jit(solution)/shard_map/store/pallas_call | solution.py:709
